TPU v7x, 512 devices: a whole 4x4x16 slice. The times are simulated.
512 devices in a mesh: rep: 32 (over z, x_lo), fsdp: 16 (over y, x_hi, core).
Axes of the slice: x: 4 (x_hi: 2, x_lo: 2; x = x_hi * 2 + x_lo), y: 4, z: 16, core: 2. Of those that a mesh axis runs over, the one named last changes fastest.
Arguments:
- tokens: bfloat16 [32, 2048, 8192], P('rep', 'fsdp'), may hold values from -6 to 6
- key_weight: bfloat16 [32, 1024, 8192], P('rep', None, 'fsdp'), may hold values from -0.0625 to 0.0625
- upstream: bfloat16 [32, 2048, 1024], P('rep', 'fsdp'), may hold values from -6 to 6
- fragment_local: bfloat16 [32, 8, 8, 8192], P('rep', None, None, 'fsdp'), may hold values from -6 to 6
- anchor: float32 [8, 8, 8192], P(None, None, 'fsdp'), may hold values from -6 to 6
- outer_velocity: float32 [8, 8, 8192], P(None, None, 'fsdp'), may hold values from -4 to 4
- fragment_pick: int32 [8], replicated, may hold values from 0 to 7, each once
Outputs:
- keys: bfloat16 [32, 2048, 1024], P('rep', 'fsdp')
- key_grad: bfloat16 [32, 1024, 8192], P('rep', None, 'fsdp')
- new_local: bfloat16 [32, 8, 8, 8192], P('rep', None, None, 'fsdp')
- new_anchor: float32 [8, 8, 8192], P(None, None, 'fsdp')
- new_velocity: float32 [8, 8, 8192], P(None, None, 'fsdp')
Inputs may be any that keep to these rules, and one draw needn't show every extreme that they name: `fragment_pick`: a permutation of the 8 fragment indices; its first entry is the fragment whose outer gradient is averaged and applied.
All inputs are finite; a program needn't handle non-finite values.
Results may differ from a plain program's by a relative error of at most 0.019.
Values may be sent and summed in bfloat16 or wider, within the bound.
No kernel may reach another device: no remote copies, remote signals or barrier semaphores. Data moves between devices by JAX's collectives and lax.ppermute only.
A program may use at most 64 MiB of HBM per device.

v0:
```python
import jax
import jax.numpy as jnp
from jax import lax
from jax.sharding import PartitionSpec as P

momentum_rate = 0.9
outer_rate = 0.7
merge_weight = 0.5


def local(tokens, key_weight, upstream, fragment_local, anchor, outer_velocity, fragment_pick):
    inputs = tokens[0]
    weight = key_weight[0]
    arriving = upstream[0]
    count = inputs.shape[0]
    scale = (count * lax.axis_size("fsdp")) ** (-0.5)
    token_columns = lax.all_to_all(inputs, "fsdp", split_axis=1, concat_axis=0, tiled=True)
    block = token_columns
    key_rows = lax.psum_scatter(
        jnp.einsum("tc,kc->tk", block, weight, preferred_element_type=jnp.float32).astype(
            jnp.bfloat16
        ),
        "fsdp",
        scatter_dimension=0,
        tiled=True,
    )
    cotangent = (arriving.astype(jnp.float32) * scale).astype(jnp.bfloat16)
    block = token_columns
    grad = jnp.einsum(
        "tk,tc->kc",
        lax.all_gather(cotangent, "fsdp", axis=0, tiled=True),
        block,
        preferred_element_type=jnp.float32,
    )
    key_grad = grad.astype(jnp.bfloat16)[None]
    pick = fragment_pick[0]
    replicas = lax.axis_size("rep")
    anchor_now = lax.dynamic_index_in_dim(anchor, pick, 0, keepdims=False)
    velocity_now = lax.dynamic_index_in_dim(outer_velocity, pick, 0, keepdims=False)
    local_now = lax.dynamic_index_in_dim(fragment_local[0], pick, 0, keepdims=False).astype(
        jnp.float32
    )
    difference = anchor_now - local_now
    delta = lax.psum(difference, "rep") / replicas
    velocity_new = momentum_rate * velocity_now + delta
    anchor_new = anchor_now - outer_rate * (delta + momentum_rate * velocity_new)
    local_new = (merge_weight * local_now + (1.0 - merge_weight) * anchor_new).astype(jnp.bfloat16)
    new_local = lax.dynamic_update_index_in_dim(fragment_local[0], local_new, pick, 0)
    new_anchor = lax.dynamic_update_index_in_dim(anchor, anchor_new, pick, 0)
    new_velocity = lax.dynamic_update_index_in_dim(outer_velocity, velocity_new, pick, 0)
    return (key_rows[None], key_grad, new_local[None], new_anchor, new_velocity)


def solution(mesh):
    return jax.shard_map(
        local,
        mesh=mesh,
        in_specs=(
            P("rep", "fsdp", None),
            P("rep", None, "fsdp"),
            P("rep", "fsdp", None),
            P("rep", None, None, "fsdp"),
            P(None, None, "fsdp"),
            P(None, None, "fsdp"),
            P(),
        ),
        out_specs=(
            P("rep", "fsdp", None),
            P("rep", None, "fsdp"),
            P("rep", None, None, "fsdp"),
            P(None, None, "fsdp"),
            P(None, None, "fsdp"),
        ),
        check_vma=False,
    )
```

profile of v0, /device:TPU:8, one launch (start us, length us, event | category | flops | bytes accessed | tf_op | source)
XLA Modules:
  0.0 210.0 jit_solution(8955108836323510290)
XLA Ops:
  7.2 0.0 copy-start
  7.2 0.0 all-gather.3.cloned.1.call-start
  7.2 0.9 copy.20
  8.1 0.9 copy.22
  9.1 0.9 copy.21
  10.0 1.7 multiply_convert_fusion
  11.7 0.0 all-gather.3.cloned.1.call-update
  11.7 0.0 reduce-scatter.2.cloned.1.call-start
  11.7 4.1 %copy.12 = bf16[1,128,8192]{1,2,0:T(8,128)(2,1)} copy(bf16[1,128,8192]{2,1,0:T(8,128)(2,1)} %param.7) | data formatting | bytes 4194304 | tf_op args[0]
  15.8 38.8 %all_to_all.19 = bf16[128,16,512]{0,2,1:T(8,128)(2,1)S(1)} all-to-all(bf16[128,16,512]{0,2,1:T(8,128)(2,1)} %bitcast.42), channel_id=1, replica_groups=mesh['rep'=32,'fsdp'=16] {'fsdp'}, dimensions={1} | all-to-all | bytes 4194304 | tf_op jit(solution)/shard_map/all_to_all | solution.py:17
  54.6 2.6 %copy.13 = bf16[16,128,512]{2,1,0:T(8,128)(2,1)} copy(bf16[16,128,512]{1,2,0:T(8,128)(2,1)S(1)} %bitcast.41) | data formatting | bytes 4194304 | tf_op jit(solution)/shard_map/all_to_all | solution.py:17
  57.2 5.9 %convolution_convert_fusion = bf16[2048,1024]{1,0:T(8,128)(2,1)} fusion(bf16[2048,512]{1,0:T(8,128)(2,1)} %bitcast.43, bf16[1,1024,512]{2,1,0:T(8,128)(2,1)S(1)} %copy-done), kind=kOutput, calls=%fused_computation.2 | convolution fusion | flops 2149580800 | bytes 7340032 | tf_op jit(solution)/shard_map/tc,kc->tk/dot_general | solution.py:20
  63.2 0.0 reduce-scatter.2.cloned.1.call-update
  63.2 0.6 copy-done.5
  64.0 126.6 %psum.7 = f32[8,512]{1,0:T(8,128)S(1)} all-reduce(f32[8,512]{1,0:T(8,128)S(1)} %convert_subtract_fusion), channel_id=1, replica_groups=mesh['rep'=32,'fsdp'=16] {'rep'}, use_global_device_ids=true, to_apply=%region_1.2 | all-reduce | flops 4096 | bytes 32768 | tf_op jit(solution)/shard_map/psum | solution.py:44
  190.6 0.0 copy-start.4
  190.6 0.0 copy-start.2
  190.6 0.0 copy-start.3
  190.6 0.0 all-gather.3.cloned.1.call-done
  190.6 0.0 copy-done.1
  190.7 5.6 %fusion.5 = bf16[1,1024,512]{2,1,0:T(8,128)(2,1)} fusion(bf16[2048,512]{1,0:T(8,128)(2,1)S(1)} %bitcast.44, bf16[1,2048,1024]{2,1,0:T(8,128)(2,1)} %all-gather.3.cloned.1.call-done), kind=kOutput, calls=%fused_computation.4 | convolution fusion | flops 2148007936 | bytes 7340032 | tf_op jit(solution)/shard_map/tk,tc->kc/dot_general | solution.py:29
  196.2 0.0 copy-done.4
  196.2 0.0 copy-done.3
  196.2 6.9 %reduce-scatter.2.cloned.1.call-done = bf16[128,1024]{1,0:T(8,128)(2,1)} async-done(((bf16[2048,1024]{1,0:T(8,128)(2,1)}), bf16[128,1024]{1,0:T(8,128)(2,1)}) %reduce-scatter.2.cloned.1.call-update) | async-done | bytes 262160 | tf_op jit(solution)/shard_map/reduce_scatter | solution.py:19
  (9 shorter events, 0.1 us)
Async XLA Ops:
  7.2 50.1 %copy-start = (bf16[1,1024,512]{2,1,0:T(8,128)(2,1)S(1)}, bf16[1,1024,512]{2,1,0:T(8,128)(2,1)}, u32[]{:S(2)}) copy-start(bf16[1,1024,512]{2,1,0:T(8,128)(2,1)} %param.8) | copy-start | bytes 3145732
  7.2 183.5 %all-gather.3.cloned.1.call-start = ((), (), s32[]{:S(2)}) async-start(), calls=%async_computation.3 | async-start | bytes 4456448 | tf_op jit(solution)/shard_map/all_gather | solution.py:31
  11.7 191.5 %reduce-scatter.2.cloned.1.call-start = ((), (), s32[]{:S(2)}) async-start(), calls=%async_computation.2 | async-start | bytes 4456448 | tf_op jit(solution)/shard_map/reduce_scatter | solution.py:19
  63.2 0.7 copy-start.5
  63.2 127.5 %copy-start.1 = (bf16[16,128,512]{2,1,0:T(8,128)(2,1)S(1)}, bf16[16,128,512]{2,1,0:T(8,128)(2,1)}, u32[]{:S(2)}) copy-start(bf16[16,128,512]{2,1,0:T(8,128)(2,1)} %copy.13) | copy-start | bytes 6291460
  190.6 5.7 %copy-start.4 = (bf16[1,8,8,512]{3,2,1,0:T(8,128)(2,1)}, bf16[1,8,8,512]{3,2,1,0:T(8,128)(2,1)S(1)}, u32[]{:S(2)}) copy-start(bf16[1,8,8,512]{3,2,1,0:T(8,128)(2,1)S(1)} %get-tuple-element.5) | copy-start | bytes 196612
  190.6 5.6 %copy-start.2 = (f32[8,8,512]{2,1,0:T(8,128)}, f32[8,8,512]{2,1,0:T(8,128)S(1)}, u32[]{:S(2)}) copy-start(f32[8,8,512]{2,1,0:T(8,128)S(1)} %get-tuple-element.7) | copy-start | bytes 393220
  190.6 5.6 %copy-start.3 = (f32[8,8,512]{2,1,0:T(8,128)}, f32[8,8,512]{2,1,0:T(8,128)S(1)}, u32[]{:S(2)}) copy-start(f32[8,8,512]{2,1,0:T(8,128)S(1)} %get-tuple-element.8) | copy-start | bytes 393220
Sparse Core Ops, SparseCore 0:
  11.9 82.5 all-gather.2
  100.0 103.1 reduce-scatter.1
where the time goes:
time: 210 us
  blocking collectives  165 us (79%)
  between operations  14.2 us (7%)
  matrix products  11.5 us (5%)
  local copies, waits for them, and re-layouts  10.1 us (5%)
  waiting for transfers between devices  6.95 us (3%)
    psum x1, blocking collectives, local(): delta = lax.psum(difference, 'rep') / replicas  127 us
    all_to_all x1, blocking collectives, local(): lax.all_to_all(inputs, 'fsdp', split_axis=1, concat_axis=0, tiled=True)  38.8 us
    unnamed x16, local copies, waits for them, and re-layouts  7.48 us
    reduce_scatter x1, waiting for transfers between devices, local(): lax.psum_scatter(jnp.einsum('tc,kc->tk', block, weight, preferred_element...  6.89 us
    dot_general x1, matrix products, local(): jnp.einsum('tc,kc->tk', block, weight, preferred_element_type=jnp.float32)  5.95 us
    dot_general x1, matrix products, local(): jnp.einsum('tk,tc->kc', lax.all_gather(cotangent, 'fsdp', axis=0, tiled=T...  5.58 us
  transfers between devices with their start and end apart: 2, of which 1 were waited for; matrix products, arithmetic and copies ran while one was open for 9% of the time, Pallas kernels for 0%

commit v1 on v0

v1 whole, which is shorter than its diff:
```python
import functools

import jax
import jax.numpy as jnp
from jax import lax
from jax.experimental import pallas as pl
from jax.experimental.pallas import tpu as pltpu
from jax.sharding import PartitionSpec as P

momentum_rate = 0.9
outer_rate = 0.7
merge_weight = 0.5

GROUP = 16
SEATS = 4
ROWS = 4
SAME_SEAT = [[row * SEATS + seat for row in range(ROWS)] for seat in range(SEATS)]


def flip(bits):
    return [(i, i ^ bits) for i in range(GROUP)]


def send(value, pairs):
    return lax.ppermute(value, "fsdp", pairs)


def exchange(value):
    return lax.all_to_all(value, "fsdp", 0, 0, axis_index_groups=SAME_SEAT)


def after(value, *others):
    return lax.optimization_barrier((value, *others))[0]


def pack_kernel(scale, cuts, tokens, upstream, *outs):
    width = tokens.shape[1]
    piece = width // GROUP
    seat = lax.rem(lax.axis_index("fsdp"), SEATS)
    cot = (upstream[...].astype(jnp.float32) * scale).astype(jnp.bfloat16)
    for chunk, (low, high) in enumerate(cuts):
        part = high - low
        out = outs[chunk]
        for row in range(ROWS):
            for k in range(SEATS):
                start = pl.multiple_of((row * SEATS + (seat ^ k)) * piece + low, 128)
                out[row, :, k * part : (k + 1) * part] = tokens[:, pl.ds(start, part)]
            if chunk == 0:
                out[row, :, SEATS * part :] = cot


def pack(tokens, upstream, scale, cuts, block=32):
    count, width = tokens.shape
    features = upstream.shape[1]
    cols = [SEATS * (high - low) + (0 if low else features) for low, high in cuts]
    return pl.pallas_call(
        functools.partial(pack_kernel, scale, cuts),
        grid=(count // block,),
        out_shape=[jax.ShapeDtypeStruct((ROWS, count, c), jnp.bfloat16) for c in cols],
        in_specs=[
            pl.BlockSpec((block, width), lambda i: (i, 0)),
            pl.BlockSpec((block, features), lambda i: (i, 0)),
        ],
        out_specs=[pl.BlockSpec((ROWS, block, c), lambda i: (0, i, 0)) for c in cols],
        cost_estimate=pl.CostEstimate(flops=0, bytes_accessed=6 << 20, transcendentals=0),
        name="pack",
    )(tokens, upstream)


def update_kernel(replicas, pick, total, frags, anchor, velocity, new_frags, new_anchor, new_velocity):
    new_frags[...] = frags[...]
    new_anchor[...] = anchor[...]
    new_velocity[...] = velocity[...]
    f = pick[0]
    delta = total[...] / replicas
    velocity_new = momentum_rate * velocity[f] + delta
    anchor_new = anchor[f] - outer_rate * (delta + momentum_rate * velocity_new)
    merged = merge_weight * frags[f].astype(jnp.float32) + (1.0 - merge_weight) * anchor_new
    new_frags[f] = merged.astype(jnp.bfloat16)
    new_anchor[f] = anchor_new
    new_velocity[f] = velocity_new


def update(replicas, pick, total, frags, anchor, velocity):
    return pl.pallas_call(
        functools.partial(update_kernel, replicas),
        out_shape=[jax.ShapeDtypeStruct(a.shape, a.dtype) for a in (frags, anchor, velocity)],
        in_specs=[pl.BlockSpec(memory_space=pltpu.SMEM)] + [pl.BlockSpec(memory_space=pltpu.VMEM)] * 4,
        out_specs=[pl.BlockSpec(memory_space=pltpu.VMEM)] * 3,
        name="update",
    )(pick, total, frags, anchor, velocity)


def local(tokens, key_weight, upstream, fragment_local, anchor, outer_velocity, fragment_pick):
    inputs = tokens[0]
    weight = key_weight[0]
    count, _ = inputs.shape
    features, piece = weight.shape
    scale = (count * lax.axis_size("fsdp")) ** (-0.5)
    (message,) = pack(inputs, upstream[0], scale, ((0, piece),))

    replicas = lax.axis_size("rep")
    pick = fragment_pick[0]
    anchor_now = lax.dynamic_index_in_dim(anchor, pick, 0, keepdims=False)
    local_now = lax.dynamic_index_in_dim(fragment_local[0], pick, 0, keepdims=False)

    def double(total, bit):
        return total + lax.ppermute(total, "rep", [(i, i ^ bit) for i in range(replicas)])

    got = exchange(message)
    weight_x = send(weight, flip(2))
    total = double(after(anchor_now - local_now.astype(jnp.float32), message), 16)
    total = double(total, 8)
    total, weight_x = lax.optimization_barrier((total, weight_x))
    total = double(total, 1)
    weight_c = send(after(weight, message), flip(1))
    weight_xc = send(weight_x, flip(1))
    got = after(got, weight_c, weight_xc, total)

    got = got.reshape(ROWS * count, -1)
    cot = got[:, SEATS * piece :]

    def grad(k):
        return jnp.einsum("tk,tc->kc", cot, got[:, k * piece : (k + 1) * piece], preferred_element_type=jnp.float32)

    far = send(grad(3).astype(jnp.bfloat16), flip(1))
    other = (grad(2) + far.astype(jnp.float32)).astype(jnp.bfloat16)
    other = send(other, flip(2))
    near = send(grad(1).astype(jnp.bfloat16), flip(1))

    weights = jnp.concatenate([weight, weight_c, weight_x, weight_xc], axis=1)
    partial = jnp.einsum("tc,kc->tk", got[:, : SEATS * piece], weights, preferred_element_type=jnp.float32)
    partial = partial.astype(jnp.bfloat16)
    keys = exchange(partial.reshape(ROWS, count, features))
    keys = jnp.sum(keys.astype(jnp.float32), axis=0).astype(jnp.bfloat16)

    total = double(double(after(total, partial), 4), 2)
    new_local, new_anchor, new_velocity = update(
        replicas, fragment_pick, total, fragment_local[0], anchor, outer_velocity
    )
    other = after(other, total, keys)
    own = (grad(0) + near.astype(jnp.float32) + other.astype(jnp.float32)).astype(jnp.bfloat16)
    return (keys[None], own[None], new_local[None], new_anchor, new_velocity)


def solution(mesh):
    return jax.shard_map(
        local,
        mesh=mesh,
        in_specs=(
            P("rep", "fsdp", None),
            P("rep", None, "fsdp"),
            P("rep", "fsdp", None),
            P("rep", None, None, "fsdp"),
            P(None, None, "fsdp"),
            P(None, None, "fsdp"),
            P(),
        ),
        out_specs=(
            P("rep", "fsdp", None),
            P("rep", None, "fsdp"),
            P("rep", None, None, "fsdp"),
            P(None, None, "fsdp"),
            P(None, None, "fsdp"),
        ),
        check_vma=False,
    )
```

time: 210 us -> 92.7 us (0.44)
  blocking collectives: 165 us -> 0 us
  starting transfers between devices: 0.08 us -> 55.8 us
  between operations: 14.2 us -> 0.9 us
  local copies, waits for them, and re-layouts: 10.1 us -> 0.98 us
  Pallas kernels: 0 us -> 5.84 us
  waiting for transfers between devices: 6.95 us -> 11.8 us
  other arithmetic: 1.74 us -> 5.23 us
    psum x1 -> x0, blocking collectives: 127 us -> none  [local(): delta = lax.psum(difference, 'rep') / replicas]
    ppermute x0 -> x11, starting transfers between devices: none -> 41.4 us  [the longest x5 27.3 us: double(): lax.ppermute(total, 'rep', [(i, i ^ bit) for i in range(replicas)])]
    all_to_all x1 -> x0, blocking collectives: 38.8 us -> none  [local(): lax.all_to_all(inputs, 'fsdp', split_axis=1, concat_axis=0, tiled=True)]
    all_to_all x0 -> x2, starting transfers between devices: none -> 14.4 us  [exchange(): return lax.all_to_all(value, 'fsdp', 0, 0, axis_index_groups=SAME_SEAT)]
    ppermute x0 -> x11, waiting for transfers between devices: none -> 11.8 us  [the longest x5 11.8 us: double(): lax.ppermute(total, 'rep', [(i, i ^ bit) for i in range(replicas)])]
    reduce_scatter x1 -> x0, waiting for transfers between devices: 6.89 us -> none  [local(): lax.psum_scatter(jnp.einsum('tc,kc->tk', block, weight, preferred_element...]
    unnamed x16 -> x10, local copies, waits for them, and re-layouts: 7.48 us -> 0.98 us
    pallas_call x0 -> x2, Pallas kernels: none -> 5.84 us  [the longest x1 4.06 us: pack(): pl.pallas_call(functools.partial(pack_kernel, scale, cuts), grid=(count /...]
  transfers between devices with their start and end apart: 2 -> 13, of which waited for: 1 -> 5; matrix products, arithmetic and copies ran while one was open for 9% -> 14% of each run, Pallas kernels for 0% -> 2%
where the time goes in v1:
time: 92.7 us; the launch traced here: 91.9 us
  starting transfers between devices  55.8 us (60%)
  waiting for transfers between devices  11.8 us (13%)
  matrix products  11.3 us (12%)
  Pallas kernels  5.84 us (6%)
  other arithmetic  5.23 us (6%)
  local copies, waits for them, and re-layouts  0.98 us (1%)
    ppermute x5, starting transfers between devices, double(): lax.ppermute(total, 'rep', [(i, i ^ bit) for i in range(replicas)])  27.3 us
    all_to_all x2, starting transfers between devices, exchange(): return lax.all_to_all(value, 'fsdp', 0, 0, axis_index_groups=SAME_SEAT)  14.4 us
    ppermute x6, starting transfers between devices, send(): return lax.ppermute(value, 'fsdp', pairs)  14.1 us
    ppermute x5, waiting for transfers between devices, double(): lax.ppermute(total, 'rep', [(i, i ^ bit) for i in range(replicas)])  11.8 us
    dot_general x4, matrix products, grad(): jnp.einsum('tk,tc->kc', cot, got[:, k * piece:(k + 1) * piece], preferred...  6.4 us
    dot_general x1, matrix products, local(): jnp.einsum('tc,kc->tk', got[:, :SEATS * piece], weights, preferred_elemen...  4.91 us
    pallas_call x1, Pallas kernels, pack(): pl.pallas_call(functools.partial(pack_kernel, scale, cuts), grid=(count /...  4.06 us
    broadcast_in_dim x1, other arithmetic, local(): return (keys[None], own[None], new_local[None], new_anchor, new_velocity)  2.94 us
  transfers between devices with their start and end apart: 13, of which 5 were waited for; matrix products, arithmetic and copies ran while one was open for 14% of the time, Pallas kernels for 2%

profile of v1, /device:TPU:8, one launch (start us, length us, event | category | flops | bytes accessed | tf_op | source)
XLA Modules:
  0.0 91.9 jit_solution(16267164736775091734)
XLA Ops:
  0.6 4.1 %pack.1 = bf16[4,128,3072]{2,1,0:T(8,128)(2,1)} custom-call(bf16[128,8192]{1,0:T(8,128)(2,1)} %bitcast.22, bf16[128,1024]{1,0:T(8,128)(2,1)} %bitcast.25), custom_call_target="tpu_custom_call" | custom-call | bytes 6291456 | tf_op jit(solution)/shard_map/pack/pallas_call | solution.py:56
  4.7 9.6 %all-to-all-start = ((bf16[4,128,3072]{2,1,0:T(8,128)(2,1)}), bf16[4,128,3072]{2,1,0:T(8,128)(2,1)S(1)}, u32[]{:S(2)}, u32[]{:S(2)}) async-start(bf16[4,128,3072]{2,1,0:T(8,128)(2,1)} %pack.1), calls=%async_computation | async-start | bytes 6291456 | tf_op jit(solution)/shard_map/all_to_all | solution.py:29
  14.3 1.9 %collective-permute-start.3 = (bf16[1024,512]{1,0:T(8,128)(2,1)}, bf16[1024,512]{1,0:T(8,128)(2,1)}, u32[]{:S(2)}, u32[]{:S(2)}) collective-permute-start(bf16[1024,512]{1,0:T(8,128)(2,1)} %bitcast.30), channel_id=1, source_target_pairs={{0,2},{1,3},{2,0},{3,1},{4,6},{5,7},{6,4},{7,5},{8,10},{9,11},{10,... | collective-permute-start | bytes 3145736 | tf_op jit(solution)/shard_map/ppermute | solution.py:25
  17.1 14.1 %collective-permute-start.1 = (f32[8,512]{1,0:T(8,128)S(1)}, f32[8,512]{1,0:T(8,128)S(1)}, u32[]{:S(2)}, u32[]{:S(2)}) collective-permute-start(f32[8,512]{1,0:T(8,128)S(1)} %convert_subtract_fusion), channel_id=1, source_target_pairs={{0,256},{16,272},{32,288},{48,304},{64,320},{80,336},{96,352},{112... | collective-permute-start | bytes 49160 | tf_op jit(solution)/shard_map/ppermute | solution.py:108
  31.2 1.7 %collective-permute-done.1 = f32[8,512]{1,0:T(8,128)S(1)} collective-permute-done((f32[8,512]{1,0:T(8,128)S(1)}, f32[8,512]{1,0:T(8,128)S(1)}, u32[]{:S(2)}, u32[]{:S(2)}) %collective-permute-start.1) | collective-permute-done | bytes 16416 | tf_op jit(solution)/shard_map/ppermute | solution.py:108
  32.9 6.0 %collective-permute-start.2 = (f32[8,512]{1,0:T(8,128)S(1)}, f32[8,512]{1,0:T(8,128)S(1)}, u32[]{:S(2)}, u32[]{:S(2)}) collective-permute-start(f32[8,512]{1,0:T(8,128)S(1)} %add.31), channel_id=1, source_target_pairs={{0,128},{16,144},{32,160},{48,176},{64,192},{80,208},{96,224},{112... | collective-permute-start | bytes 49160 | tf_op jit(solution)/shard_map/ppermute | solution.py:108
  39.0 1.9 %collective-permute-start = (bf16[1024,512]{1,0:T(8,128)(2,1)}, bf16[1024,512]{1,0:T(8,128)(2,1)S(1)}, u32[]{:S(2)}, u32[]{:S(2)}) collective-permute-start(bf16[1024,512]{1,0:T(8,128)(2,1)} %bitcast.31), channel_id=1, source_target_pairs={{0,1},{1,0},{2,3},{3,2},{4,5},{5,4},{6,7},{7,6},{8,9},{9,8},{10,11... | collective-permute-start | bytes 3145736 | tf_op jit(solution)/shard_map/ppermute | solution.py:25
  42.5 1.9 %collective-permute-start.4 = (bf16[1024,512]{1,0:T(8,128)(2,1)}, bf16[1024,512]{1,0:T(8,128)(2,1)}, u32[]{:S(2)}, u32[]{:S(2)}) collective-permute-start(bf16[1024,512]{1,0:T(8,128)(2,1)} %collective-permute-done.3), channel_id=1, source_target_pairs={{0,1},{1,0},{2,3},{3,2},{4,5},{5,4},{6,7},{7,6},{8,9},{9,8},{10,11... | collective-permute-start | bytes 3145736 | tf_op jit(solution)/shard_map/ppermute | solution.py:25
  44.4 2.5 %collective-permute-start.5 = (f32[8,512]{1,0:T(8,128)S(1)}, f32[8,512]{1,0:T(8,128)S(1)}, u32[]{:S(2)}, u32[]{:S(2)}) collective-permute-start(f32[8,512]{1,0:T(8,128)S(1)} %add.32), channel_id=1, source_target_pairs={{0,16},{16,0},{32,48},{48,32},{64,80},{80,64},{96,112},{112,96},{1... | collective-permute-start | bytes 49160 | tf_op jit(solution)/shard_map/ppermute | solution.py:108
  46.9 3.1 %collective-permute-done.5 = f32[8,512]{1,0:T(8,128)S(1)} collective-permute-done((f32[8,512]{1,0:T(8,128)S(1)}, f32[8,512]{1,0:T(8,128)S(1)}, u32[]{:S(2)}, u32[]{:S(2)}) %collective-permute-start.5) | collective-permute-done | bytes 16416 | tf_op jit(solution)/shard_map/ppermute | solution.py:108
  51.8 1.9 %collective-permute-start.7 = (bf16[1024,512]{1,0:T(8,128)(2,1)S(1)}, bf16[1024,512]{1,0:T(8,128)(2,1)S(1)}, u32[]{:S(2)}, u32[]{:S(2)}) collective-permute-start(bf16[1024,512]{1,0:T(8,128)(2,1)S(1)} %convolution_convert_fusion), channel_id=1, source_target_pairs={{0,1},{1,0},{2,3},{3,2},{4,5},{5,4},{6,7},{7,6},{8,9},{9,8},{10,11... | collective-permute-start | bytes 3145736 | tf_op jit(solution)/shard_map/ppermute | solution.py:25
  53.7 1.8 %convolution_convert_fusion.1 = bf16[1024,512]{1,0:T(8,128)(2,1)} fusion(bf16[512,3072]{1,0:T(8,128)(2,1)S(1)} %bitcast.18), kind=kOutput, calls=%fused_computation.13 | convolution fusion | flops 537395200 | bytes 2621440 | tf_op jit(solution)/shard_map/tk,tc->kc/dot_general | solution.py:124
  55.5 2.5 %collective-permute-start.6 = (bf16[1024,512]{1,0:T(8,128)(2,1)}, bf16[1024,512]{1,0:T(8,128)(2,1)}, u32[]{:S(2)}, u32[]{:S(2)}) collective-permute-start(bf16[1024,512]{1,0:T(8,128)(2,1)} %convolution_convert_fusion.1), channel_id=1, source_target_pairs={{0,1},{1,0},{2,3},{3,2},{4,5},{5,4},{6,7},{7,6},{8,9},{9,8},{10,11... | collective-permute-start | bytes 3145736 | tf_op jit(solution)/shard_map/ppermute | solution.py:25
  58.0 1.8 %add_convert_fusion.1 = bf16[1024,512]{1,0:T(8,128)(2,1)} fusion(bf16[1024,512]{1,0:T(8,128)(2,1)S(1)} %collective-permute-done.7, bf16[512,3072]{1,0:T(8,128)(2,1)S(1)} %bitcast.19), kind=kOutput, calls=%fused_computation.10 | convolution fusion | flops 538443776 | bytes 3670016 | tf_op jit(solution)/shard_map/tk,tc->kc/dot_general | solution.py:124
  59.8 3.9 %collective-permute-start.8 = (bf16[1024,512]{1,0:T(8,128)(2,1)}, bf16[1024,512]{1,0:T(8,128)(2,1)}, u32[]{:S(2)}, u32[]{:S(2)}) collective-permute-start(bf16[1024,512]{1,0:T(8,128)(2,1)} %add_convert_fusion.1), channel_id=1, source_target_pairs={{0,2},{1,3},{2,0},{3,1},{4,6},{5,7},{6,4},{7,5},{8,10},{9,11},{10,... | collective-permute-start | bytes 3145736 | tf_op jit(solution)/shard_map/ppermute | solution.py:25
  63.7 4.9 %fusion.9 = bf16[512,1024]{1,0:T(8,128)(2,1)} fusion(bf16[1024,512]{1,0:T(8,128)(2,1)} %collective-permute-done.4, bf16[1024,512]{1,0:T(8,128)(2,1)} %collective-permute-done.3, bf16[1024,512]{1,0:T(8,128)(2,1)S(1)} %copy-done.4, bf16[1024,512]{1,0:T(8,128)(2,1)S(1)} %bitcast.32, bf16[512,3072]{1,0:T(8,128)(2,1)S(1)} %bitcast.20), kind=kOutput, calls=%fused_computation.11 | convolution fusion | flops 2164785152 | bytes 7340032 | tf_op jit(solution)/shard_map/tc,kc->tk/dot_general | solution.py:132
  68.7 4.8 %all-to-all-start.1 = ((bf16[4,128,1024]{2,1,0:T(8,128)(2,1)}), bf16[4,128,1024]{2,1,0:T(8,128)(2,1)S(1)}, u32[]{:S(2)}, u32[]{:S(2)}) async-start(bf16[4,128,1024]{2,1,0:T(8,128)(2,1)} %bitcast.23), calls=%async_computation.1 | async-start | bytes 2097152 | tf_op jit(solution)/shard_map/all_to_all | solution.py:29
  73.4 2.7 %collective-permute-start.9 = (f32[8,512]{1,0:T(8,128)S(1)}, f32[8,512]{1,0:T(8,128)S(1)}, u32[]{:S(2)}, u32[]{:S(2)}) collective-permute-start(f32[8,512]{1,0:T(8,128)S(1)} %add.33), channel_id=1, source_target_pairs={{0,64},{16,80},{32,96},{48,112},{64,0},{80,16},{96,32},{112,48},{1... | collective-permute-start | bytes 49160 | tf_op jit(solution)/shard_map/ppermute | solution.py:108
  76.1 3.8 %collective-permute-done.9 = f32[8,512]{1,0:T(8,128)S(1)} collective-permute-done((f32[8,512]{1,0:T(8,128)S(1)}, f32[8,512]{1,0:T(8,128)S(1)}, u32[]{:S(2)}, u32[]{:S(2)}) %collective-permute-start.9) | collective-permute-done | bytes 16416 | tf_op jit(solution)/shard_map/ppermute | solution.py:108
  80.0 1.9 %collective-permute-start.10 = (f32[8,512]{1,0:T(8,128)S(1)}, f32[8,512]{1,0:T(8,128)S(1)}, u32[]{:S(2)}, u32[]{:S(2)}) collective-permute-start(f32[8,512]{1,0:T(8,128)S(1)} %add.36), channel_id=1, source_target_pairs={{0,32},{16,48},{32,0},{48,16},{64,96},{80,112},{96,64},{112,80},{1... | collective-permute-start | bytes 49160 | tf_op jit(solution)/shard_map/ppermute | solution.py:108
  81.9 2.1 %fusion.19 = f32[1024,512]{1,0:T(8,128)S(1)} fusion(bf16[512,3072]{1,0:T(8,128)(2,1)} %bitcast.21), kind=kOutput, calls=%fused_computation.19 | convolution fusion | flops 536870912 | bytes 3670016 | tf_op jit(solution)/shard_map/tk,tc->kc/dot_general | solution.py:124
  84.0 1.6 %collective-permute-done.10 = f32[8,512]{1,0:T(8,128)S(1)} collective-permute-done((f32[8,512]{1,0:T(8,128)S(1)}, f32[8,512]{1,0:T(8,128)S(1)}, u32[]{:S(2)}, u32[]{:S(2)}) %collective-permute-start.10) | collective-permute-done | bytes 16416 | tf_op jit(solution)/shard_map/ppermute | solution.py:108
  86.2 1.8 %update.1 = (bf16[8,8,512]{2,1,0:T(8,128)(2,1)}, f32[8,8,512]{2,1,0:T(8,128)}, f32[8,8,512]{2,1,0:T(8,128)}) custom-call(s32[8]{0:T(128)} %pick.1, f32[8,512]{1,0:T(8,128)} %add.37.total, bf16[8,8,512]{2,1,0:T(8,128)(2,1)} %bitcast.26, f32[8,8,512]{2,1,0:T(8,128)} %anchor.1, f32[8,8,512]{2,1,0:T(8,128)} %velocity.1), custom_call_target="tpu_custom_call" | custom-call | tf_op jit(solution)/shard_map/update/pallas_call | solution.py:85
  88.9 2.9 %fusion.14 = bf16[1,1024,512]{2,1,0:T(8,128)(2,1)} fusion(bf16[1024,512]{1,0:T(8,128)(2,1)} %collective-permute-done.8, f32[1024,512]{1,0:T(8,128)S(1)} %fusion.19, bf16[1024,512]{1,0:T(8,128)(2,1)} %collective-permute-done.6), kind=kLoop, calls=%fused_computation.14 | loop fusion | flops 2621440 | bytes 5242880 | tf_op jit(solution)/shard_map/broadcast_in_dim | solution.py:143
  (27 shorter events, 5.6 us)
Async XLA Ops:
  4.7 11.5 %copy-start.1 = (s32[8]{0:T(128)S(1)}, s32[8]{0:T(128)}, u32[]{:S(2)}) copy-start(s32[8]{0:T(128)} %pick.1) | copy-start | bytes 100
  4.7 46.3 %all-to-all-start = ((bf16[4,128,3072]{2,1,0:T(8,128)(2,1)}), bf16[4,128,3072]{2,1,0:T(8,128)(2,1)S(1)}, u32[]{:S(2)}, u32[]{:S(2)}) async-start(bf16[4,128,3072]{2,1,0:T(8,128)(2,1)} %pack.1), calls=%async_computation | async-start | bytes 6291456 | tf_op jit(solution)/shard_map/all_to_all | solution.py:29
  14.3 28.2 %collective-permute-start.3 = (bf16[1024,512]{1,0:T(8,128)(2,1)}, bf16[1024,512]{1,0:T(8,128)(2,1)}, u32[]{:S(2)}, u32[]{:S(2)}) collective-permute-start(bf16[1024,512]{1,0:T(8,128)(2,1)} %bitcast.30), channel_id=1, source_target_pairs={{0,2},{1,3},{2,0},{3,1},{4,6},{5,7},{6,4},{7,5},{8,10},{9,11},{10,... | collective-permute-start | bytes 3145736 | tf_op jit(solution)/shard_map/ppermute | solution.py:25
  17.1 15.9 %collective-permute-start.1 = (f32[8,512]{1,0:T(8,128)S(1)}, f32[8,512]{1,0:T(8,128)S(1)}, u32[]{:S(2)}, u32[]{:S(2)}) collective-permute-start(f32[8,512]{1,0:T(8,128)S(1)} %convert_subtract_fusion), channel_id=1, source_target_pairs={{0,256},{16,272},{32,288},{48,304},{64,320},{80,336},{96,352},{112... | collective-permute-start | bytes 49160 | tf_op jit(solution)/shard_map/ppermute | solution.py:108
  32.9 9.5 %collective-permute-start.2 = (f32[8,512]{1,0:T(8,128)S(1)}, f32[8,512]{1,0:T(8,128)S(1)}, u32[]{:S(2)}, u32[]{:S(2)}) collective-permute-start(f32[8,512]{1,0:T(8,128)S(1)} %add.31), channel_id=1, source_target_pairs={{0,128},{16,144},{32,160},{48,176},{64,192},{80,208},{96,224},{112... | collective-permute-start | bytes 49160 | tf_op jit(solution)/shard_map/ppermute | solution.py:108
  39.0 11.1 %collective-permute-start = (bf16[1024,512]{1,0:T(8,128)(2,1)}, bf16[1024,512]{1,0:T(8,128)(2,1)S(1)}, u32[]{:S(2)}, u32[]{:S(2)}) collective-permute-start(bf16[1024,512]{1,0:T(8,128)(2,1)} %bitcast.31), channel_id=1, source_target_pairs={{0,1},{1,0},{2,3},{3,2},{4,5},{5,4},{6,7},{7,6},{8,9},{9,8},{10,11... | collective-permute-start | bytes 3145736 | tf_op jit(solution)/shard_map/ppermute | solution.py:25
  42.5 8.5 %collective-permute-start.4 = (bf16[1024,512]{1,0:T(8,128)(2,1)}, bf16[1024,512]{1,0:T(8,128)(2,1)}, u32[]{:S(2)}, u32[]{:S(2)}) collective-permute-start(bf16[1024,512]{1,0:T(8,128)(2,1)} %collective-permute-done.3), channel_id=1, source_target_pairs={{0,1},{1,0},{2,3},{3,2},{4,5},{5,4},{6,7},{7,6},{8,9},{9,8},{10,11... | collective-permute-start | bytes 3145736 | tf_op jit(solution)/shard_map/ppermute | solution.py:25
  44.4 5.6 %collective-permute-start.5 = (f32[8,512]{1,0:T(8,128)S(1)}, f32[8,512]{1,0:T(8,128)S(1)}, u32[]{:S(2)}, u32[]{:S(2)}) collective-permute-start(f32[8,512]{1,0:T(8,128)S(1)} %add.32), channel_id=1, source_target_pairs={{0,16},{16,0},{32,48},{48,32},{64,80},{80,64},{96,112},{112,96},{1... | collective-permute-start | bytes 49160 | tf_op jit(solution)/shard_map/ppermute | solution.py:108
  50.1 1.0 %copy-start.3 = (bf16[1024,512]{1,0:T(8,128)(2,1)}, bf16[1024,512]{1,0:T(8,128)(2,1)S(1)}, u32[]{:S(2)}) copy-start(bf16[1024,512]{1,0:T(8,128)(2,1)S(1)} %collective-permute-done) | copy-start | bytes 3145732
  51.0 12.7 %copy-start = (bf16[4,128,3072]{2,1,0:T(8,128)(2,1)}, bf16[4,128,3072]{2,1,0:T(8,128)(2,1)S(1)}, u32[]{:S(2)}) copy-start(bf16[4,128,3072]{2,1,0:T(8,128)(2,1)S(1)} %all-to-all-done) | copy-start | bytes 9437188
  51.8 6.2 %collective-permute-start.7 = (bf16[1024,512]{1,0:T(8,128)(2,1)S(1)}, bf16[1024,512]{1,0:T(8,128)(2,1)S(1)}, u32[]{:S(2)}, u32[]{:S(2)}) collective-permute-start(bf16[1024,512]{1,0:T(8,128)(2,1)S(1)} %convolution_convert_fusion), channel_id=1, source_target_pairs={{0,1},{1,0},{2,3},{3,2},{4,5},{5,4},{6,7},{7,6},{8,9},{9,8},{10,11... | collective-permute-start | bytes 3145736 | tf_op jit(solution)/shard_map/ppermute | solution.py:25
  55.5 8.3 %copy-start.2 = (bf16[1,1024,512]{2,1,0:T(8,128)(2,1)S(1)}, bf16[1,1024,512]{2,1,0:T(8,128)(2,1)}, u32[]{:S(2)}) copy-start(bf16[1,1024,512]{2,1,0:T(8,128)(2,1)} %param.8) | copy-start | bytes 3145732
  55.5 8.3 %copy-start.4 = (bf16[1024,512]{1,0:T(8,128)(2,1)S(1)}, bf16[1024,512]{1,0:T(8,128)(2,1)}, u32[]{:S(2)}) copy-start(bf16[1024,512]{1,0:T(8,128)(2,1)} %copy-done.3) | copy-start | bytes 3145732
  55.5 33.5 %collective-permute-start.6 = (bf16[1024,512]{1,0:T(8,128)(2,1)}, bf16[1024,512]{1,0:T(8,128)(2,1)}, u32[]{:S(2)}, u32[]{:S(2)}) collective-permute-start(bf16[1024,512]{1,0:T(8,128)(2,1)} %convolution_convert_fusion.1), channel_id=1, source_target_pairs={{0,1},{1,0},{2,3},{3,2},{4,5},{5,4},{6,7},{7,6},{8,9},{9,8},{10,11... | collective-permute-start | bytes 3145736 | tf_op jit(solution)/shard_map/ppermute | solution.py:25
  59.8 29.1 %collective-permute-start.8 = (bf16[1024,512]{1,0:T(8,128)(2,1)}, bf16[1024,512]{1,0:T(8,128)(2,1)}, u32[]{:S(2)}, u32[]{:S(2)}) collective-permute-start(bf16[1024,512]{1,0:T(8,128)(2,1)} %add_convert_fusion.1), channel_id=1, source_target_pairs={{0,2},{1,3},{2,0},{3,1},{4,6},{5,7},{6,4},{7,5},{8,10},{9,11},{10,... | collective-permute-start | bytes 3145736 | tf_op jit(solution)/shard_map/ppermute | solution.py:25
  68.7 19.3 %all-to-all-start.1 = ((bf16[4,128,1024]{2,1,0:T(8,128)(2,1)}), bf16[4,128,1024]{2,1,0:T(8,128)(2,1)S(1)}, u32[]{:S(2)}, u32[]{:S(2)}) async-start(bf16[4,128,1024]{2,1,0:T(8,128)(2,1)} %bitcast.23), calls=%async_computation.1 | async-start | bytes 2097152 | tf_op jit(solution)/shard_map/all_to_all | solution.py:29
  73.4 6.5 %collective-permute-start.9 = (f32[8,512]{1,0:T(8,128)S(1)}, f32[8,512]{1,0:T(8,128)S(1)}, u32[]{:S(2)}, u32[]{:S(2)}) collective-permute-start(f32[8,512]{1,0:T(8,128)S(1)} %add.33), channel_id=1, source_target_pairs={{0,64},{16,80},{32,96},{48,112},{64,0},{80,16},{96,32},{112,48},{1... | collective-permute-start | bytes 49160 | tf_op jit(solution)/shard_map/ppermute | solution.py:108
  80.0 5.6 %collective-permute-start.10 = (f32[8,512]{1,0:T(8,128)S(1)}, f32[8,512]{1,0:T(8,128)S(1)}, u32[]{:S(2)}, u32[]{:S(2)}) collective-permute-start(f32[8,512]{1,0:T(8,128)S(1)} %add.36), channel_id=1, source_target_pairs={{0,32},{16,48},{32,0},{48,16},{64,96},{80,112},{96,64},{112,80},{1... | collective-permute-start | bytes 49160 | tf_op jit(solution)/shard_map/ppermute | solution.py:108

commit v2 on v1

--- a/solution.py
+++ b/solution.py
@@ -49,7 +49,7 @@
                 out[row, :, SEATS * part :] = cot
 
 
-def pack(tokens, upstream, scale, cuts, block=32):
+def pack(tokens, upstream, scale, cuts, block=64):
     count, width = tokens.shape
     features = upstream.shape[1]
     cols = [SEATS * (high - low) + (0 if low else features) for low, high in cuts]

time: 92.7 us -> 91.6 us (0.988)
  Pallas kernels: 5.84 us -> 4.81 us
    pallas_call x1, Pallas kernels: 4.06 us -> 3.03 us  [pack(): pl.pallas_call(functools.partial(pack_kernel, scale, cuts), grid=(count /...]
where the time goes in v2:
time: 91.6 us; the launch traced here: 90.8 us
  starting transfers between devices  55.8 us (61%)
  waiting for transfers between devices  11.8 us (13%)
  matrix products  11.3 us (12%)
  other arithmetic  5.23 us (6%)
  Pallas kernels  4.81 us (5%)
  local copies, waits for them, and re-layouts  0.98 us (1%)
    ppermute x5, starting transfers between devices, double(): lax.ppermute(total, 'rep', [(i, i ^ bit) for i in range(replicas)])  27.3 us
    all_to_all x2, starting transfers between devices, exchange(): return lax.all_to_all(value, 'fsdp', 0, 0, axis_index_groups=SAME_SEAT)  14.4 us
    ppermute x6, starting transfers between devices, send(): return lax.ppermute(value, 'fsdp', pairs)  14.1 us
    ppermute x5, waiting for transfers between devices, double(): lax.ppermute(total, 'rep', [(i, i ^ bit) for i in range(replicas)])  11.8 us
    dot_general x4, matrix products, grad(): jnp.einsum('tk,tc->kc', cot, got[:, k * piece:(k + 1) * piece], preferred...  6.39 us
    dot_general x1, matrix products, local(): jnp.einsum('tc,kc->tk', got[:, :SEATS * piece], weights, preferred_elemen...  4.9 us
    pallas_call x1, Pallas kernels, pack(): pl.pallas_call(functools.partial(pack_kernel, scale, cuts), grid=(count /...  3.03 us
    broadcast_in_dim x1, other arithmetic, local(): return (keys[None], own[None], new_local[None], new_anchor, new_velocity)  2.94 us
  transfers between devices with their start and end apart: 13, of which 5 were waited for; matrix products, arithmetic and copies ran while one was open for 14% of the time, Pallas kernels for 2%

profile of v2, /device:TPU:8, one launch (start us, length us, event | category | flops | bytes accessed | tf_op | source)
XLA Modules:
  0.0 90.8 jit_solution(9284398335354478063)
XLA Ops:
  0.6 3.0 %pack.1 = bf16[4,128,3072]{2,1,0:T(8,128)(2,1)} custom-call(bf16[128,8192]{1,0:T(8,128)(2,1)} %bitcast.22, bf16[128,1024]{1,0:T(8,128)(2,1)} %bitcast.25), custom_call_target="tpu_custom_call" | custom-call | bytes 6291456 | tf_op jit(solution)/shard_map/pack/pallas_call | solution.py:56
  3.7 9.6 %all-to-all-start = ((bf16[4,128,3072]{2,1,0:T(8,128)(2,1)}), bf16[4,128,3072]{2,1,0:T(8,128)(2,1)S(1)}, u32[]{:S(2)}, u32[]{:S(2)}) async-start(bf16[4,128,3072]{2,1,0:T(8,128)(2,1)} %pack.1), calls=%async_computation | async-start | bytes 6291456 | tf_op jit(solution)/shard_map/all_to_all | solution.py:29
  13.3 1.9 %collective-permute-start.3 = (bf16[1024,512]{1,0:T(8,128)(2,1)}, bf16[1024,512]{1,0:T(8,128)(2,1)}, u32[]{:S(2)}, u32[]{:S(2)}) collective-permute-start(bf16[1024,512]{1,0:T(8,128)(2,1)} %bitcast.30), channel_id=1, source_target_pairs={{0,2},{1,3},{2,0},{3,1},{4,6},{5,7},{6,4},{7,5},{8,10},{9,11},{10,... | collective-permute-start | bytes 3145736 | tf_op jit(solution)/shard_map/ppermute | solution.py:25
  16.0 14.1 %collective-permute-start.1 = (f32[8,512]{1,0:T(8,128)S(1)}, f32[8,512]{1,0:T(8,128)S(1)}, u32[]{:S(2)}, u32[]{:S(2)}) collective-permute-start(f32[8,512]{1,0:T(8,128)S(1)} %convert_subtract_fusion), channel_id=1, source_target_pairs={{0,256},{16,272},{32,288},{48,304},{64,320},{80,336},{96,352},{112... | collective-permute-start | bytes 49160 | tf_op jit(solution)/shard_map/ppermute | solution.py:108
  30.2 1.7 %collective-permute-done.1 = f32[8,512]{1,0:T(8,128)S(1)} collective-permute-done((f32[8,512]{1,0:T(8,128)S(1)}, f32[8,512]{1,0:T(8,128)S(1)}, u32[]{:S(2)}, u32[]{:S(2)}) %collective-permute-start.1) | collective-permute-done | bytes 16416 | tf_op jit(solution)/shard_map/ppermute | solution.py:108
  31.9 6.0 %collective-permute-start.2 = (f32[8,512]{1,0:T(8,128)S(1)}, f32[8,512]{1,0:T(8,128)S(1)}, u32[]{:S(2)}, u32[]{:S(2)}) collective-permute-start(f32[8,512]{1,0:T(8,128)S(1)} %add.31), channel_id=1, source_target_pairs={{0,128},{16,144},{32,160},{48,176},{64,192},{80,208},{96,224},{112... | collective-permute-start | bytes 49160 | tf_op jit(solution)/shard_map/ppermute | solution.py:108
  37.9 1.9 %collective-permute-start = (bf16[1024,512]{1,0:T(8,128)(2,1)}, bf16[1024,512]{1,0:T(8,128)(2,1)S(1)}, u32[]{:S(2)}, u32[]{:S(2)}) collective-permute-start(bf16[1024,512]{1,0:T(8,128)(2,1)} %bitcast.31), channel_id=1, source_target_pairs={{0,1},{1,0},{2,3},{3,2},{4,5},{5,4},{6,7},{7,6},{8,9},{9,8},{10,11... | collective-permute-start | bytes 3145736 | tf_op jit(solution)/shard_map/ppermute | solution.py:25
  41.4 1.9 %collective-permute-start.4 = (bf16[1024,512]{1,0:T(8,128)(2,1)}, bf16[1024,512]{1,0:T(8,128)(2,1)}, u32[]{:S(2)}, u32[]{:S(2)}) collective-permute-start(bf16[1024,512]{1,0:T(8,128)(2,1)} %collective-permute-done.3), channel_id=1, source_target_pairs={{0,1},{1,0},{2,3},{3,2},{4,5},{5,4},{6,7},{7,6},{8,9},{9,8},{10,11... | collective-permute-start | bytes 3145736 | tf_op jit(solution)/shard_map/ppermute | solution.py:25
  43.4 2.5 %collective-permute-start.5 = (f32[8,512]{1,0:T(8,128)S(1)}, f32[8,512]{1,0:T(8,128)S(1)}, u32[]{:S(2)}, u32[]{:S(2)}) collective-permute-start(f32[8,512]{1,0:T(8,128)S(1)} %add.32), channel_id=1, source_target_pairs={{0,16},{16,0},{32,48},{48,32},{64,80},{80,64},{96,112},{112,96},{1... | collective-permute-start | bytes 49160 | tf_op jit(solution)/shard_map/ppermute | solution.py:108
  45.9 3.1 %collective-permute-done.5 = f32[8,512]{1,0:T(8,128)S(1)} collective-permute-done((f32[8,512]{1,0:T(8,128)S(1)}, f32[8,512]{1,0:T(8,128)S(1)}, u32[]{:S(2)}, u32[]{:S(2)}) %collective-permute-start.5) | collective-permute-done | bytes 16416 | tf_op jit(solution)/shard_map/ppermute | solution.py:108
  50.7 1.9 %collective-permute-start.7 = (bf16[1024,512]{1,0:T(8,128)(2,1)S(1)}, bf16[1024,512]{1,0:T(8,128)(2,1)S(1)}, u32[]{:S(2)}, u32[]{:S(2)}) collective-permute-start(bf16[1024,512]{1,0:T(8,128)(2,1)S(1)} %convolution_convert_fusion), channel_id=1, source_target_pairs={{0,1},{1,0},{2,3},{3,2},{4,5},{5,4},{6,7},{7,6},{8,9},{9,8},{10,11... | collective-permute-start | bytes 3145736 | tf_op jit(solution)/shard_map/ppermute | solution.py:25
  52.7 1.8 %convolution_convert_fusion.1 = bf16[1024,512]{1,0:T(8,128)(2,1)} fusion(bf16[512,3072]{1,0:T(8,128)(2,1)S(1)} %bitcast.18), kind=kOutput, calls=%fused_computation.13 | convolution fusion | flops 537395200 | bytes 2621440 | tf_op jit(solution)/shard_map/tk,tc->kc/dot_general | solution.py:124
  54.4 2.5 %collective-permute-start.6 = (bf16[1024,512]{1,0:T(8,128)(2,1)}, bf16[1024,512]{1,0:T(8,128)(2,1)}, u32[]{:S(2)}, u32[]{:S(2)}) collective-permute-start(bf16[1024,512]{1,0:T(8,128)(2,1)} %convolution_convert_fusion.1), channel_id=1, source_target_pairs={{0,1},{1,0},{2,3},{3,2},{4,5},{5,4},{6,7},{7,6},{8,9},{9,8},{10,11... | collective-permute-start | bytes 3145736 | tf_op jit(solution)/shard_map/ppermute | solution.py:25
  57.0 1.8 %add_convert_fusion.1 = bf16[1024,512]{1,0:T(8,128)(2,1)} fusion(bf16[1024,512]{1,0:T(8,128)(2,1)S(1)} %collective-permute-done.7, bf16[512,3072]{1,0:T(8,128)(2,1)S(1)} %bitcast.19), kind=kOutput, calls=%fused_computation.10 | convolution fusion | flops 538443776 | bytes 3670016 | tf_op jit(solution)/shard_map/tk,tc->kc/dot_general | solution.py:124
  58.8 3.9 %collective-permute-start.8 = (bf16[1024,512]{1,0:T(8,128)(2,1)}, bf16[1024,512]{1,0:T(8,128)(2,1)}, u32[]{:S(2)}, u32[]{:S(2)}) collective-permute-start(bf16[1024,512]{1,0:T(8,128)(2,1)} %add_convert_fusion.1), channel_id=1, source_target_pairs={{0,2},{1,3},{2,0},{3,1},{4,6},{5,7},{6,4},{7,5},{8,10},{9,11},{10,... | collective-permute-start | bytes 3145736 | tf_op jit(solution)/shard_map/ppermute | solution.py:25
  62.7 4.9 %fusion.9 = bf16[512,1024]{1,0:T(8,128)(2,1)} fusion(bf16[1024,512]{1,0:T(8,128)(2,1)} %collective-permute-done.4, bf16[1024,512]{1,0:T(8,128)(2,1)} %collective-permute-done.3, bf16[1024,512]{1,0:T(8,128)(2,1)S(1)} %copy-done.4, bf16[1024,512]{1,0:T(8,128)(2,1)S(1)} %bitcast.32, bf16[512,3072]{1,0:T(8,128)(2,1)S(1)} %bitcast.20), kind=kOutput, calls=%fused_computation.11 | convolution fusion | flops 2164785152 | bytes 7340032 | tf_op jit(solution)/shard_map/tc,kc->tk/dot_general | solution.py:132
  67.6 4.8 %all-to-all-start.1 = ((bf16[4,128,1024]{2,1,0:T(8,128)(2,1)}), bf16[4,128,1024]{2,1,0:T(8,128)(2,1)S(1)}, u32[]{:S(2)}, u32[]{:S(2)}) async-start(bf16[4,128,1024]{2,1,0:T(8,128)(2,1)} %bitcast.23), calls=%async_computation.1 | async-start | bytes 2097152 | tf_op jit(solution)/shard_map/all_to_all | solution.py:29
  72.4 2.7 %collective-permute-start.9 = (f32[8,512]{1,0:T(8,128)S(1)}, f32[8,512]{1,0:T(8,128)S(1)}, u32[]{:S(2)}, u32[]{:S(2)}) collective-permute-start(f32[8,512]{1,0:T(8,128)S(1)} %add.33), channel_id=1, source_target_pairs={{0,64},{16,80},{32,96},{48,112},{64,0},{80,16},{96,32},{112,48},{1... | collective-permute-start | bytes 49160 | tf_op jit(solution)/shard_map/ppermute | solution.py:108
  75.1 3.8 %collective-permute-done.9 = f32[8,512]{1,0:T(8,128)S(1)} collective-permute-done((f32[8,512]{1,0:T(8,128)S(1)}, f32[8,512]{1,0:T(8,128)S(1)}, u32[]{:S(2)}, u32[]{:S(2)}) %collective-permute-start.9) | collective-permute-done | bytes 16416 | tf_op jit(solution)/shard_map/ppermute | solution.py:108
  78.9 1.9 %collective-permute-start.10 = (f32[8,512]{1,0:T(8,128)S(1)}, f32[8,512]{1,0:T(8,128)S(1)}, u32[]{:S(2)}, u32[]{:S(2)}) collective-permute-start(f32[8,512]{1,0:T(8,128)S(1)} %add.36), channel_id=1, source_target_pairs={{0,32},{16,48},{32,0},{48,16},{64,96},{80,112},{96,64},{112,80},{1... | collective-permute-start | bytes 49160 | tf_op jit(solution)/shard_map/ppermute | solution.py:108
  80.9 2.1 %fusion.19 = f32[1024,512]{1,0:T(8,128)S(1)} fusion(bf16[512,3072]{1,0:T(8,128)(2,1)} %bitcast.21), kind=kOutput, calls=%fused_computation.19 | convolution fusion | flops 536870912 | bytes 3670016 | tf_op jit(solution)/shard_map/tk,tc->kc/dot_general | solution.py:124
  83.0 1.6 %collective-permute-done.10 = f32[8,512]{1,0:T(8,128)S(1)} collective-permute-done((f32[8,512]{1,0:T(8,128)S(1)}, f32[8,512]{1,0:T(8,128)S(1)}, u32[]{:S(2)}, u32[]{:S(2)}) %collective-permute-start.10) | collective-permute-done | bytes 16416 | tf_op jit(solution)/shard_map/ppermute | solution.py:108
  85.2 1.8 %update.1 = (bf16[8,8,512]{2,1,0:T(8,128)(2,1)}, f32[8,8,512]{2,1,0:T(8,128)}, f32[8,8,512]{2,1,0:T(8,128)}) custom-call(s32[8]{0:T(128)} %pick.1, f32[8,512]{1,0:T(8,128)} %add.37.total, bf16[8,8,512]{2,1,0:T(8,128)(2,1)} %bitcast.26, f32[8,8,512]{2,1,0:T(8,128)} %anchor.1, f32[8,8,512]{2,1,0:T(8,128)} %velocity.1), custom_call_target="tpu_custom_call" | custom-call | tf_op jit(solution)/shard_map/update/pallas_call | solution.py:85
  87.9 2.9 %fusion.14 = bf16[1,1024,512]{2,1,0:T(8,128)(2,1)} fusion(bf16[1024,512]{1,0:T(8,128)(2,1)} %collective-permute-done.8, f32[1024,512]{1,0:T(8,128)S(1)} %fusion.19, bf16[1024,512]{1,0:T(8,128)(2,1)} %collective-permute-done.6), kind=kLoop, calls=%fused_computation.14 | loop fusion | flops 2621440 | bytes 5242880 | tf_op jit(solution)/shard_map/broadcast_in_dim | solution.py:143
  (27 shorter events, 5.6 us)
Async XLA Ops:
  3.7 11.5 %copy-start.1 = (s32[8]{0:T(128)S(1)}, s32[8]{0:T(128)}, u32[]{:S(2)}) copy-start(s32[8]{0:T(128)} %pick.1) | copy-start | bytes 100
  3.7 46.3 %all-to-all-start = ((bf16[4,128,3072]{2,1,0:T(8,128)(2,1)}), bf16[4,128,3072]{2,1,0:T(8,128)(2,1)S(1)}, u32[]{:S(2)}, u32[]{:S(2)}) async-start(bf16[4,128,3072]{2,1,0:T(8,128)(2,1)} %pack.1), calls=%async_computation | async-start | bytes 6291456 | tf_op jit(solution)/shard_map/all_to_all | solution.py:29
  13.3 28.2 %collective-permute-start.3 = (bf16[1024,512]{1,0:T(8,128)(2,1)}, bf16[1024,512]{1,0:T(8,128)(2,1)}, u32[]{:S(2)}, u32[]{:S(2)}) collective-permute-start(bf16[1024,512]{1,0:T(8,128)(2,1)} %bitcast.30), channel_id=1, source_target_pairs={{0,2},{1,3},{2,0},{3,1},{4,6},{5,7},{6,4},{7,5},{8,10},{9,11},{10,... | collective-permute-start | bytes 3145736 | tf_op jit(solution)/shard_map/ppermute | solution.py:25
  16.0 15.9 %collective-permute-start.1 = (f32[8,512]{1,0:T(8,128)S(1)}, f32[8,512]{1,0:T(8,128)S(1)}, u32[]{:S(2)}, u32[]{:S(2)}) collective-permute-start(f32[8,512]{1,0:T(8,128)S(1)} %convert_subtract_fusion), channel_id=1, source_target_pairs={{0,256},{16,272},{32,288},{48,304},{64,320},{80,336},{96,352},{112... | collective-permute-start | bytes 49160 | tf_op jit(solution)/shard_map/ppermute | solution.py:108
  31.9 9.5 %collective-permute-start.2 = (f32[8,512]{1,0:T(8,128)S(1)}, f32[8,512]{1,0:T(8,128)S(1)}, u32[]{:S(2)}, u32[]{:S(2)}) collective-permute-start(f32[8,512]{1,0:T(8,128)S(1)} %add.31), channel_id=1, source_target_pairs={{0,128},{16,144},{32,160},{48,176},{64,192},{80,208},{96,224},{112... | collective-permute-start | bytes 49160 | tf_op jit(solution)/shard_map/ppermute | solution.py:108
  37.9 11.1 %collective-permute-start = (bf16[1024,512]{1,0:T(8,128)(2,1)}, bf16[1024,512]{1,0:T(8,128)(2,1)S(1)}, u32[]{:S(2)}, u32[]{:S(2)}) collective-permute-start(bf16[1024,512]{1,0:T(8,128)(2,1)} %bitcast.31), channel_id=1, source_target_pairs={{0,1},{1,0},{2,3},{3,2},{4,5},{5,4},{6,7},{7,6},{8,9},{9,8},{10,11... | collective-permute-start | bytes 3145736 | tf_op jit(solution)/shard_map/ppermute | solution.py:25
  41.4 8.5 %collective-permute-start.4 = (bf16[1024,512]{1,0:T(8,128)(2,1)}, bf16[1024,512]{1,0:T(8,128)(2,1)}, u32[]{:S(2)}, u32[]{:S(2)}) collective-permute-start(bf16[1024,512]{1,0:T(8,128)(2,1)} %collective-permute-done.3), channel_id=1, source_target_pairs={{0,1},{1,0},{2,3},{3,2},{4,5},{5,4},{6,7},{7,6},{8,9},{9,8},{10,11... | collective-permute-start | bytes 3145736 | tf_op jit(solution)/shard_map/ppermute | solution.py:25
  43.4 5.6 %collective-permute-start.5 = (f32[8,512]{1,0:T(8,128)S(1)}, f32[8,512]{1,0:T(8,128)S(1)}, u32[]{:S(2)}, u32[]{:S(2)}) collective-permute-start(f32[8,512]{1,0:T(8,128)S(1)} %add.32), channel_id=1, source_target_pairs={{0,16},{16,0},{32,48},{48,32},{64,80},{80,64},{96,112},{112,96},{1... | collective-permute-start | bytes 49160 | tf_op jit(solution)/shard_map/ppermute | solution.py:108
  49.0 1.0 %copy-start.3 = (bf16[1024,512]{1,0:T(8,128)(2,1)}, bf16[1024,512]{1,0:T(8,128)(2,1)S(1)}, u32[]{:S(2)}) copy-start(bf16[1024,512]{1,0:T(8,128)(2,1)S(1)} %collective-permute-done) | copy-start | bytes 3145732
  50.0 12.7 %copy-start = (bf16[4,128,3072]{2,1,0:T(8,128)(2,1)}, bf16[4,128,3072]{2,1,0:T(8,128)(2,1)S(1)}, u32[]{:S(2)}) copy-start(bf16[4,128,3072]{2,1,0:T(8,128)(2,1)S(1)} %all-to-all-done) | copy-start | bytes 9437188
  50.7 6.2 %collective-permute-start.7 = (bf16[1024,512]{1,0:T(8,128)(2,1)S(1)}, bf16[1024,512]{1,0:T(8,128)(2,1)S(1)}, u32[]{:S(2)}, u32[]{:S(2)}) collective-permute-start(bf16[1024,512]{1,0:T(8,128)(2,1)S(1)} %convolution_convert_fusion), channel_id=1, source_target_pairs={{0,1},{1,0},{2,3},{3,2},{4,5},{5,4},{6,7},{7,6},{8,9},{9,8},{10,11... | collective-permute-start | bytes 3145736 | tf_op jit(solution)/shard_map/ppermute | solution.py:25
  54.4 8.3 %copy-start.2 = (bf16[1,1024,512]{2,1,0:T(8,128)(2,1)S(1)}, bf16[1,1024,512]{2,1,0:T(8,128)(2,1)}, u32[]{:S(2)}) copy-start(bf16[1,1024,512]{2,1,0:T(8,128)(2,1)} %param.8) | copy-start | bytes 3145732
  54.4 8.3 %copy-start.4 = (bf16[1024,512]{1,0:T(8,128)(2,1)S(1)}, bf16[1024,512]{1,0:T(8,128)(2,1)}, u32[]{:S(2)}) copy-start(bf16[1024,512]{1,0:T(8,128)(2,1)} %copy-done.3) | copy-start | bytes 3145732
  54.4 33.5 %collective-permute-start.6 = (bf16[1024,512]{1,0:T(8,128)(2,1)}, bf16[1024,512]{1,0:T(8,128)(2,1)}, u32[]{:S(2)}, u32[]{:S(2)}) collective-permute-start(bf16[1024,512]{1,0:T(8,128)(2,1)} %convolution_convert_fusion.1), channel_id=1, source_target_pairs={{0,1},{1,0},{2,3},{3,2},{4,5},{5,4},{6,7},{7,6},{8,9},{9,8},{10,11... | collective-permute-start | bytes 3145736 | tf_op jit(solution)/shard_map/ppermute | solution.py:25
  58.8 29.1 %collective-permute-start.8 = (bf16[1024,512]{1,0:T(8,128)(2,1)}, bf16[1024,512]{1,0:T(8,128)(2,1)}, u32[]{:S(2)}, u32[]{:S(2)}) collective-permute-start(bf16[1024,512]{1,0:T(8,128)(2,1)} %add_convert_fusion.1), channel_id=1, source_target_pairs={{0,2},{1,3},{2,0},{3,1},{4,6},{5,7},{6,4},{7,5},{8,10},{9,11},{10,... | collective-permute-start | bytes 3145736 | tf_op jit(solution)/shard_map/ppermute | solution.py:25
  67.6 19.3 %all-to-all-start.1 = ((bf16[4,128,1024]{2,1,0:T(8,128)(2,1)}), bf16[4,128,1024]{2,1,0:T(8,128)(2,1)S(1)}, u32[]{:S(2)}, u32[]{:S(2)}) async-start(bf16[4,128,1024]{2,1,0:T(8,128)(2,1)} %bitcast.23), calls=%async_computation.1 | async-start | bytes 2097152 | tf_op jit(solution)/shard_map/all_to_all | solution.py:29
  72.4 6.5 %collective-permute-start.9 = (f32[8,512]{1,0:T(8,128)S(1)}, f32[8,512]{1,0:T(8,128)S(1)}, u32[]{:S(2)}, u32[]{:S(2)}) collective-permute-start(f32[8,512]{1,0:T(8,128)S(1)} %add.33), channel_id=1, source_target_pairs={{0,64},{16,80},{32,96},{48,112},{64,0},{80,16},{96,32},{112,48},{1... | collective-permute-start | bytes 49160 | tf_op jit(solution)/shard_map/ppermute | solution.py:108
  78.9 5.6 %collective-permute-start.10 = (f32[8,512]{1,0:T(8,128)S(1)}, f32[8,512]{1,0:T(8,128)S(1)}, u32[]{:S(2)}, u32[]{:S(2)}) collective-permute-start(f32[8,512]{1,0:T(8,128)S(1)} %add.36), channel_id=1, source_target_pairs={{0,32},{16,48},{32,0},{48,16},{64,96},{80,112},{96,64},{112,80},{1... | collective-permute-start | bytes 49160 | tf_op jit(solution)/shard_map/ppermute | solution.py:108

commit v3 on v2

--- a/solution.py
+++ b/solution.py
@@ -91,6 +91,59 @@
     )(pick, total, frags, anchor, velocity)
 
 
+def finish_kernel(base, other, parts, own, keys, held, result, held_parts, held_keys, sems, out_sems):
+    chunks, rows = held.shape[:2]
+    blocks, amount, tall = held_parts.shape[:3]
+    copies = [(other.at[pl.ds(c * rows, rows)], held.at[c]) for c in range(chunks)]
+    copies += [(parts.at[:, pl.ds(n * tall, tall)], held_parts.at[n]) for n in range(blocks)]
+    copies = [pltpu.make_async_copy(source, to, sems.at[n]) for n, (source, to) in enumerate(copies)]
+    for copy in copies:
+        copy.start()
+    outs = []
+
+    def leave(source, to):
+        outs.append(pltpu.make_async_copy(source, to, out_sems.at[len(outs)]))
+        outs[-1].start()
+
+    for c in range(chunks):
+        copies[c].wait()
+        part = pl.ds(c * rows, rows)
+        result[c] = (base[part] + held[c].astype(jnp.float32)).astype(jnp.bfloat16)
+        leave(result.at[c], own.at[part])
+    for n in range(blocks):
+        copies[chunks + n].wait()
+        total = held_parts[n, 0].astype(jnp.float32)
+        for part in range(1, amount):
+            total = total + held_parts[n, part].astype(jnp.float32)
+        held_keys[n] = total.astype(jnp.bfloat16)
+        leave(held_keys.at[n], keys.at[pl.ds(n * tall, tall)])
+    for copy in outs:
+        copy.wait()
+
+
+def finish(base, other, parts, chunks=4, blocks=2):
+    rows, cols = base.shape
+    amount, count, features = parts.shape
+    bf16 = jnp.bfloat16
+    return pl.pallas_call(
+        finish_kernel,
+        out_shape=[jax.ShapeDtypeStruct((rows, cols), bf16), jax.ShapeDtypeStruct((count, features), bf16)],
+        in_specs=[pl.BlockSpec(memory_space=pltpu.VMEM)] + [pl.BlockSpec(memory_space=pl.ANY)] * 2,
+        out_specs=[pl.BlockSpec(memory_space=pl.ANY)] * 2,
+        scratch_shapes=[
+            pltpu.VMEM((chunks, rows // chunks, cols), bf16),
+            pltpu.VMEM((chunks, rows // chunks, cols), bf16),
+            pltpu.VMEM((blocks, amount, count // blocks, features), bf16),
+            pltpu.VMEM((blocks, count // blocks, features), bf16),
+            pltpu.SemaphoreType.DMA((blocks + chunks,)),
+            pltpu.SemaphoreType.DMA((blocks + chunks,)),
+        ],
+        compiler_params=pltpu.CompilerParams(vmem_limit_bytes=10 << 20),
+        cost_estimate=pl.CostEstimate(flops=1 << 20, bytes_accessed=6 << 20, transcendentals=0),
+        name="finish",
+    )(base, other, parts)
+
+
 def local(tokens, key_weight, upstream, fragment_local, anchor, outer_velocity, fragment_pick):
     inputs = tokens[0]
     weight = key_weight[0]
@@ -132,14 +185,15 @@
     partial = jnp.einsum("tc,kc->tk", got[:, : SEATS * piece], weights, preferred_element_type=jnp.float32)
     partial = partial.astype(jnp.bfloat16)
     keys = exchange(partial.reshape(ROWS, count, features))
-    keys = jnp.sum(keys.astype(jnp.float32), axis=0).astype(jnp.bfloat16)
-
-    total = double(double(after(total, partial), 4), 2)
+
+    total, near, partial = lax.optimization_barrier((total, near, partial))
+    total = double(double(total, 4), 2)
+    base = grad(0) + near.astype(jnp.float32)
     new_local, new_anchor, new_velocity = update(
         replicas, fragment_pick, total, fragment_local[0], anchor, outer_velocity
     )
-    other = after(other, total, keys)
-    own = (grad(0) + near.astype(jnp.float32) + other.astype(jnp.float32)).astype(jnp.bfloat16)
+    other, keys, new_anchor = lax.optimization_barrier((other, keys, new_anchor))
+    own, keys = finish(base, other, keys)
     return (keys[None], own[None], new_local[None], new_anchor, new_velocity)
 
 

time: 91.6 us -> 90.4 us (0.987)
  other arithmetic: 5.23 us -> 1.35 us
  Pallas kernels: 4.81 us -> 6.94 us
    broadcast_in_dim x1 -> x0, other arithmetic: 2.94 us -> none  [local(): return (keys[None], own[None], new_local[None], new_anchor, new_velocity)]
    pallas_call x0 -> x1, Pallas kernels: none -> 2.14 us  [finish(): pl.pallas_call(finish_kernel, out_shape=[jax.ShapeDtypeStruct((rows, cols...]
    reduce_sum x1 -> x0, other arithmetic: 0.93 us -> none  [local(): keys = jnp.sum(keys.astype(jnp.float32), axis=0).astype(jnp.bfloat16)]
  transfers between devices with their start and end apart: 13 -> 13, of which waited for: 5 -> 6; matrix products, arithmetic and copies ran while one was open for 14% -> 14% of each run, Pallas kernels for 2% -> 2%
where the time goes in v3:
time: 90.4 us; the launch traced here: 89.7 us
  starting transfers between devices  55.8 us (62%)
  waiting for transfers between devices  11.9 us (13%)
  matrix products  11.8 us (13%)
  Pallas kernels  6.94 us (8%)
  other arithmetic  1.35 us (1%)
  local copies, waits for them, and re-layouts  1.08 us (1%)
  between operations  0.91 us (1%)
    ppermute x5, starting transfers between devices, double(): lax.ppermute(total, 'rep', [(i, i ^ bit) for i in range(replicas)])  27.3 us
    all_to_all x2, starting transfers between devices, exchange(): return lax.all_to_all(value, 'fsdp', 0, 0, axis_index_groups=SAME_SEAT)  14.4 us
    ppermute x6, starting transfers between devices, send(): return lax.ppermute(value, 'fsdp', pairs)  14.1 us
    ppermute x5, waiting for transfers between devices, double(): lax.ppermute(total, 'rep', [(i, i ^ bit) for i in range(replicas)])  11.3 us
    dot_general x4, matrix products, grad(): jnp.einsum('tk,tc->kc', cot, got[:, k * piece:(k + 1) * piece], preferred...  6.76 us
    dot_general x1, matrix products, local(): jnp.einsum('tc,kc->tk', got[:, :SEATS * piece], weights, preferred_elemen...  5.01 us
    pallas_call x1, Pallas kernels, pack(): pl.pallas_call(functools.partial(pack_kernel, scale, cuts), grid=(count /...  3.02 us
    pallas_call x1, Pallas kernels, finish(): pl.pallas_call(finish_kernel, out_shape=[jax.ShapeDtypeStruct((rows, cols...  2.14 us
  transfers between devices with their start and end apart: 13, of which 6 were waited for; matrix products, arithmetic and copies ran while one was open for 14% of the time, Pallas kernels for 2%

profile of v3, /device:TPU:8, one launch (start us, length us, event | category | flops | bytes accessed | tf_op | source)
XLA Modules:
  0.0 89.7 jit_solution(3559204792434812052)
XLA Ops:
  0.6 3.0 %pack.1 = bf16[4,128,3072]{2,1,0:T(8,128)(2,1)} custom-call(bf16[128,8192]{1,0:T(8,128)(2,1)} %bitcast.21, bf16[128,1024]{1,0:T(8,128)(2,1)} %bitcast.23), custom_call_target="tpu_custom_call" | custom-call | bytes 6291456 | tf_op jit(solution)/shard_map/pack/pallas_call | solution.py:56
  3.7 9.6 %all-to-all-start = ((bf16[4,128,3072]{2,1,0:T(8,128)(2,1)}), bf16[4,128,3072]{2,1,0:T(8,128)(2,1)S(1)}, u32[]{:S(2)}, u32[]{:S(2)}) async-start(bf16[4,128,3072]{2,1,0:T(8,128)(2,1)} %pack.1), calls=%async_computation | async-start | bytes 6291456 | tf_op jit(solution)/shard_map/all_to_all | solution.py:29
  13.3 1.9 %collective-permute-start.3 = (bf16[1024,512]{1,0:T(8,128)(2,1)}, bf16[1024,512]{1,0:T(8,128)(2,1)}, u32[]{:S(2)}, u32[]{:S(2)}) collective-permute-start(bf16[1024,512]{1,0:T(8,128)(2,1)} %bitcast.28), channel_id=1, source_target_pairs={{0,2},{1,3},{2,0},{3,1},{4,6},{5,7},{6,4},{7,5},{8,10},{9,11},{10,... | collective-permute-start | bytes 3145736 | tf_op jit(solution)/shard_map/ppermute | solution.py:25
  16.0 14.1 %collective-permute-start.1 = (f32[8,512]{1,0:T(8,128)S(1)}, f32[8,512]{1,0:T(8,128)S(1)}, u32[]{:S(2)}, u32[]{:S(2)}) collective-permute-start(f32[8,512]{1,0:T(8,128)S(1)} %convert_subtract_fusion), channel_id=1, source_target_pairs={{0,256},{16,272},{32,288},{48,304},{64,320},{80,336},{96,352},{112... | collective-permute-start | bytes 49160 | tf_op jit(solution)/shard_map/ppermute | solution.py:161
  30.2 1.7 %collective-permute-done.1 = f32[8,512]{1,0:T(8,128)S(1)} collective-permute-done((f32[8,512]{1,0:T(8,128)S(1)}, f32[8,512]{1,0:T(8,128)S(1)}, u32[]{:S(2)}, u32[]{:S(2)}) %collective-permute-start.1) | collective-permute-done | bytes 16416 | tf_op jit(solution)/shard_map/ppermute | solution.py:161
  31.9 6.0 %collective-permute-start.2 = (f32[8,512]{1,0:T(8,128)S(1)}, f32[8,512]{1,0:T(8,128)S(1)}, u32[]{:S(2)}, u32[]{:S(2)}) collective-permute-start(f32[8,512]{1,0:T(8,128)S(1)} %add.28), channel_id=1, source_target_pairs={{0,128},{16,144},{32,160},{48,176},{64,192},{80,208},{96,224},{112... | collective-permute-start | bytes 49160 | tf_op jit(solution)/shard_map/ppermute | solution.py:161
  37.9 1.9 %collective-permute-start = (bf16[1024,512]{1,0:T(8,128)(2,1)}, bf16[1024,512]{1,0:T(8,128)(2,1)S(1)}, u32[]{:S(2)}, u32[]{:S(2)}) collective-permute-start(bf16[1024,512]{1,0:T(8,128)(2,1)} %bitcast.29), channel_id=1, source_target_pairs={{0,1},{1,0},{2,3},{3,2},{4,5},{5,4},{6,7},{7,6},{8,9},{9,8},{10,11... | collective-permute-start | bytes 3145736 | tf_op jit(solution)/shard_map/ppermute | solution.py:25
  39.9 1.6 %collective-permute-done.2 = f32[8,512]{1,0:T(8,128)S(1)} collective-permute-done((f32[8,512]{1,0:T(8,128)S(1)}, f32[8,512]{1,0:T(8,128)S(1)}, u32[]{:S(2)}, u32[]{:S(2)}) %collective-permute-start.2) | collective-permute-done | bytes 16416 | tf_op jit(solution)/shard_map/ppermute | solution.py:161
  41.4 1.9 %collective-permute-start.4 = (bf16[1024,512]{1,0:T(8,128)(2,1)}, bf16[1024,512]{1,0:T(8,128)(2,1)}, u32[]{:S(2)}, u32[]{:S(2)}) collective-permute-start(bf16[1024,512]{1,0:T(8,128)(2,1)} %collective-permute-done.3), channel_id=1, source_target_pairs={{0,1},{1,0},{2,3},{3,2},{4,5},{5,4},{6,7},{7,6},{8,9},{9,8},{10,11... | collective-permute-start | bytes 3145736 | tf_op jit(solution)/shard_map/ppermute | solution.py:25
  43.4 2.5 %collective-permute-start.5 = (f32[8,512]{1,0:T(8,128)S(1)}, f32[8,512]{1,0:T(8,128)S(1)}, u32[]{:S(2)}, u32[]{:S(2)}) collective-permute-start(f32[8,512]{1,0:T(8,128)S(1)} %add.29), channel_id=1, source_target_pairs={{0,16},{16,0},{32,48},{48,32},{64,80},{80,64},{96,112},{112,96},{1... | collective-permute-start | bytes 49160 | tf_op jit(solution)/shard_map/ppermute | solution.py:161
  45.9 3.1 %collective-permute-done.5 = f32[8,512]{1,0:T(8,128)S(1)} collective-permute-done((f32[8,512]{1,0:T(8,128)S(1)}, f32[8,512]{1,0:T(8,128)S(1)}, u32[]{:S(2)}, u32[]{:S(2)}) %collective-permute-start.5) | collective-permute-done | bytes 16416 | tf_op jit(solution)/shard_map/ppermute | solution.py:161
  50.8 1.9 %collective-permute-start.7 = (bf16[1024,512]{1,0:T(8,128)(2,1)S(1)}, bf16[1024,512]{1,0:T(8,128)(2,1)S(1)}, u32[]{:S(2)}, u32[]{:S(2)}) collective-permute-start(bf16[1024,512]{1,0:T(8,128)(2,1)S(1)} %convolution_convert_fusion), channel_id=1, source_target_pairs={{0,1},{1,0},{2,3},{3,2},{4,5},{5,4},{6,7},{7,6},{8,9},{9,8},{10,11... | collective-permute-start | bytes 3145736 | tf_op jit(solution)/shard_map/ppermute | solution.py:25
  52.8 1.7 %convolution_convert_fusion.1 = bf16[1024,512]{1,0:T(8,128)(2,1)} fusion(bf16[512,3072]{1,0:T(8,128)(2,1)S(1)} %bitcast.17), kind=kOutput, calls=%fused_computation.13 | convolution fusion | flops 537395200 | bytes 2621440 | tf_op jit(solution)/shard_map/tk,tc->kc/dot_general | solution.py:177
  54.5 2.5 %collective-permute-start.6 = (bf16[1024,512]{1,0:T(8,128)(2,1)}, bf16[1024,512]{1,0:T(8,128)(2,1)}, u32[]{:S(2)}, u32[]{:S(2)}) collective-permute-start(bf16[1024,512]{1,0:T(8,128)(2,1)} %convolution_convert_fusion.1), channel_id=1, source_target_pairs={{0,1},{1,0},{2,3},{3,2},{4,5},{5,4},{6,7},{7,6},{8,9},{9,8},{10,11... | collective-permute-start | bytes 3145736 | tf_op jit(solution)/shard_map/ppermute | solution.py:25
  57.0 1.7 %add_convert_fusion = bf16[1024,512]{1,0:T(8,128)(2,1)} fusion(bf16[1024,512]{1,0:T(8,128)(2,1)S(1)} %collective-permute-done.7, bf16[512,3072]{1,0:T(8,128)(2,1)S(1)} %bitcast.18), kind=kOutput, calls=%fused_computation.9 | convolution fusion | flops 538443776 | bytes 3670016 | tf_op jit(solution)/shard_map/tk,tc->kc/dot_general | solution.py:177
  58.8 3.9 %collective-permute-start.8 = (bf16[1024,512]{1,0:T(8,128)(2,1)}, bf16[1024,512]{1,0:T(8,128)(2,1)}, u32[]{:S(2)}, u32[]{:S(2)}) collective-permute-start(bf16[1024,512]{1,0:T(8,128)(2,1)} %add_convert_fusion), channel_id=1, source_target_pairs={{0,2},{1,3},{2,0},{3,1},{4,6},{5,7},{6,4},{7,5},{8,10},{9,11},{10,... | collective-permute-start | bytes 3145736 | tf_op jit(solution)/shard_map/ppermute | solution.py:25
  62.7 5.0 %fusion.9 = bf16[512,1024]{1,0:T(8,128)(2,1)} fusion(bf16[1024,512]{1,0:T(8,128)(2,1)} %collective-permute-done.4, bf16[1024,512]{1,0:T(8,128)(2,1)} %collective-permute-done.3, bf16[1024,512]{1,0:T(8,128)(2,1)S(1)} %copy-done.4, bf16[1024,512]{1,0:T(8,128)(2,1)S(1)} %bitcast.30, bf16[512,3072]{1,0:T(8,128)(2,1)S(1)} %bitcast.19), kind=kOutput, calls=%fused_computation.11 | convolution fusion | flops 2164785152 | bytes 7340032 | tf_op jit(solution)/shard_map/tc,kc->tk/dot_general | solution.py:185
  67.7 4.8 %all-to-all-start.1 = ((bf16[4,128,1024]{2,1,0:T(8,128)(2,1)}), bf16[4,128,1024]{2,1,0:T(8,128)(2,1)S(1)}, u32[]{:S(2)}, u32[]{:S(2)}) async-start(bf16[4,128,1024]{2,1,0:T(8,128)(2,1)} %bitcast.22), calls=%async_computation.1 | async-start | bytes 2097152 | tf_op jit(solution)/shard_map/all_to_all | solution.py:29
  72.5 2.7 %collective-permute-start.9 = (f32[8,512]{1,0:T(8,128)S(1)}, f32[8,512]{1,0:T(8,128)S(1)}, u32[]{:S(2)}, u32[]{:S(2)}) collective-permute-start(f32[8,512]{1,0:T(8,128)S(1)} %add.30), channel_id=1, source_target_pairs={{0,64},{16,80},{32,96},{48,112},{64,0},{80,16},{96,32},{112,48},{1... | collective-permute-start | bytes 49160 | tf_op jit(solution)/shard_map/ppermute | solution.py:161
  75.2 3.8 %collective-permute-done.9 = f32[8,512]{1,0:T(8,128)S(1)} collective-permute-done((f32[8,512]{1,0:T(8,128)S(1)}, f32[8,512]{1,0:T(8,128)S(1)}, u32[]{:S(2)}, u32[]{:S(2)}) %collective-permute-start.9) | collective-permute-done | bytes 16416 | tf_op jit(solution)/shard_map/ppermute | solution.py:161
  79.0 1.9 %collective-permute-start.10 = (f32[8,512]{1,0:T(8,128)S(1)}, f32[8,512]{1,0:T(8,128)S(1)}, u32[]{:S(2)}, u32[]{:S(2)}) collective-permute-start(f32[8,512]{1,0:T(8,128)S(1)} %add.33), channel_id=1, source_target_pairs={{0,32},{16,48},{32,0},{48,16},{64,96},{80,112},{96,64},{112,80},{1... | collective-permute-start | bytes 49160 | tf_op jit(solution)/shard_map/ppermute | solution.py:161
  80.9 2.6 %convert_add_fusion.base = f32[1024,512]{1,0:T(8,128)S(1)} fusion(bf16[1024,512]{1,0:T(8,128)(2,1)} %collective-permute-done.6, bf16[512,3072]{1,0:T(8,128)(2,1)} %bitcast.20), kind=kOutput, calls=%fused_computation.10 | convolution fusion | flops 537919488 | bytes 4718592 | tf_op jit(solution)/shard_map/tk,tc->kc/dot_general | solution.py:177
  85.3 1.8 %update.1 = (bf16[8,8,512]{2,1,0:T(8,128)(2,1)}, f32[8,8,512]{2,1,0:T(8,128)}, f32[8,8,512]{2,1,0:T(8,128)}) custom-call(s32[8]{0:T(128)} %pick.1, f32[8,512]{1,0:T(8,128)} %add.34.total, bf16[8,8,512]{2,1,0:T(8,128)(2,1)} %bitcast.24, f32[8,8,512]{2,1,0:T(8,128)} %anchor.1, f32[8,8,512]{2,1,0:T(8,128)} %velocity.1), custom_call_target="tpu_custom_call" | custom-call | tf_op jit(solution)/shard_map/update/pallas_call | solution.py:85
  87.5 2.1 %finish.1 = (bf16[1024,512]{1,0:T(8,128)(2,1)}, bf16[128,1024]{1,0:T(8,128)(2,1)}) custom-call(f32[1024,512]{1,0:T(8,128)S(1)} %convert_add_fusion.base, bf16[1024,512]{1,0:T(8,128)(2,1)} %collective-permute-done.8.other, bf16[4,128,1024]{2,1,0:T(8,128)(2,1)S(1)} %all-to-all-done.1.parts), custom_call_target="tpu_custom_call" | custom-call | flops 1048576 | bytes 6291456 | tf_op jit(solution)/shard_map/finish/pallas_call | solution.py:128
  (26 shorter events, 4.8 us)
Async XLA Ops:
  3.7 11.5 %copy-start.1 = (s32[8]{0:T(128)S(1)}, s32[8]{0:T(128)}, u32[]{:S(2)}) copy-start(s32[8]{0:T(128)} %pick.1) | copy-start | bytes 100
  3.7 46.4 %all-to-all-start = ((bf16[4,128,3072]{2,1,0:T(8,128)(2,1)}), bf16[4,128,3072]{2,1,0:T(8,128)(2,1)S(1)}, u32[]{:S(2)}, u32[]{:S(2)}) async-start(bf16[4,128,3072]{2,1,0:T(8,128)(2,1)} %pack.1), calls=%async_computation | async-start | bytes 6291456 | tf_op jit(solution)/shard_map/all_to_all | solution.py:29
  13.3 28.2 %collective-permute-start.3 = (bf16[1024,512]{1,0:T(8,128)(2,1)}, bf16[1024,512]{1,0:T(8,128)(2,1)}, u32[]{:S(2)}, u32[]{:S(2)}) collective-permute-start(bf16[1024,512]{1,0:T(8,128)(2,1)} %bitcast.28), channel_id=1, source_target_pairs={{0,2},{1,3},{2,0},{3,1},{4,6},{5,7},{6,4},{7,5},{8,10},{9,11},{10,... | collective-permute-start | bytes 3145736 | tf_op jit(solution)/shard_map/ppermute | solution.py:25
  16.0 15.9 %collective-permute-start.1 = (f32[8,512]{1,0:T(8,128)S(1)}, f32[8,512]{1,0:T(8,128)S(1)}, u32[]{:S(2)}, u32[]{:S(2)}) collective-permute-start(f32[8,512]{1,0:T(8,128)S(1)} %convert_subtract_fusion), channel_id=1, source_target_pairs={{0,256},{16,272},{32,288},{48,304},{64,320},{80,336},{96,352},{112... | collective-permute-start | bytes 49160 | tf_op jit(solution)/shard_map/ppermute | solution.py:161
  31.9 9.5 %collective-permute-start.2 = (f32[8,512]{1,0:T(8,128)S(1)}, f32[8,512]{1,0:T(8,128)S(1)}, u32[]{:S(2)}, u32[]{:S(2)}) collective-permute-start(f32[8,512]{1,0:T(8,128)S(1)} %add.28), channel_id=1, source_target_pairs={{0,128},{16,144},{32,160},{48,176},{64,192},{80,208},{96,224},{112... | collective-permute-start | bytes 49160 | tf_op jit(solution)/shard_map/ppermute | solution.py:161
  37.9 11.1 %collective-permute-start = (bf16[1024,512]{1,0:T(8,128)(2,1)}, bf16[1024,512]{1,0:T(8,128)(2,1)S(1)}, u32[]{:S(2)}, u32[]{:S(2)}) collective-permute-start(bf16[1024,512]{1,0:T(8,128)(2,1)} %bitcast.29), channel_id=1, source_target_pairs={{0,1},{1,0},{2,3},{3,2},{4,5},{5,4},{6,7},{7,6},{8,9},{9,8},{10,11... | collective-permute-start | bytes 3145736 | tf_op jit(solution)/shard_map/ppermute | solution.py:25
  41.4 8.6 %collective-permute-start.4 = (bf16[1024,512]{1,0:T(8,128)(2,1)}, bf16[1024,512]{1,0:T(8,128)(2,1)}, u32[]{:S(2)}, u32[]{:S(2)}) collective-permute-start(bf16[1024,512]{1,0:T(8,128)(2,1)} %collective-permute-done.3), channel_id=1, source_target_pairs={{0,1},{1,0},{2,3},{3,2},{4,5},{5,4},{6,7},{7,6},{8,9},{9,8},{10,11... | collective-permute-start | bytes 3145736 | tf_op jit(solution)/shard_map/ppermute | solution.py:25
  43.4 5.6 %collective-permute-start.5 = (f32[8,512]{1,0:T(8,128)S(1)}, f32[8,512]{1,0:T(8,128)S(1)}, u32[]{:S(2)}, u32[]{:S(2)}) collective-permute-start(f32[8,512]{1,0:T(8,128)S(1)} %add.29), channel_id=1, source_target_pairs={{0,16},{16,0},{32,48},{48,32},{64,80},{80,64},{96,112},{112,96},{1... | collective-permute-start | bytes 49160 | tf_op jit(solution)/shard_map/ppermute | solution.py:161
  49.0 1.1 %copy-start.3 = (bf16[1024,512]{1,0:T(8,128)(2,1)}, bf16[1024,512]{1,0:T(8,128)(2,1)S(1)}, u32[]{:S(2)}) copy-start(bf16[1024,512]{1,0:T(8,128)(2,1)S(1)} %collective-permute-done) | copy-start | bytes 3145732
  50.1 12.6 %copy-start = (bf16[4,128,3072]{2,1,0:T(8,128)(2,1)}, bf16[4,128,3072]{2,1,0:T(8,128)(2,1)S(1)}, u32[]{:S(2)}) copy-start(bf16[4,128,3072]{2,1,0:T(8,128)(2,1)S(1)} %all-to-all-done) | copy-start | bytes 9437188
  50.8 6.2 %collective-permute-start.7 = (bf16[1024,512]{1,0:T(8,128)(2,1)S(1)}, bf16[1024,512]{1,0:T(8,128)(2,1)S(1)}, u32[]{:S(2)}, u32[]{:S(2)}) collective-permute-start(bf16[1024,512]{1,0:T(8,128)(2,1)S(1)} %convolution_convert_fusion), channel_id=1, source_target_pairs={{0,1},{1,0},{2,3},{3,2},{4,5},{5,4},{6,7},{7,6},{8,9},{9,8},{10,11... | collective-permute-start | bytes 3145736 | tf_op jit(solution)/shard_map/ppermute | solution.py:25
  54.5 8.2 %copy-start.2 = (bf16[1,1024,512]{2,1,0:T(8,128)(2,1)S(1)}, bf16[1,1024,512]{2,1,0:T(8,128)(2,1)}, u32[]{:S(2)}) copy-start(bf16[1,1024,512]{2,1,0:T(8,128)(2,1)} %param.8) | copy-start | bytes 3145732
  54.5 8.2 %copy-start.4 = (bf16[1024,512]{1,0:T(8,128)(2,1)S(1)}, bf16[1024,512]{1,0:T(8,128)(2,1)}, u32[]{:S(2)}) copy-start(bf16[1024,512]{1,0:T(8,128)(2,1)} %copy-done.3) | copy-start | bytes 3145732
  54.5 18.0 %collective-permute-start.6 = (bf16[1024,512]{1,0:T(8,128)(2,1)}, bf16[1024,512]{1,0:T(8,128)(2,1)}, u32[]{:S(2)}, u32[]{:S(2)}) collective-permute-start(bf16[1024,512]{1,0:T(8,128)(2,1)} %convolution_convert_fusion.1), channel_id=1, source_target_pairs={{0,1},{1,0},{2,3},{3,2},{4,5},{5,4},{6,7},{7,6},{8,9},{9,8},{10,11... | collective-permute-start | bytes 3145736 | tf_op jit(solution)/shard_map/ppermute | solution.py:25
  58.8 28.8 %collective-permute-start.8 = (bf16[1024,512]{1,0:T(8,128)(2,1)}, bf16[1024,512]{1,0:T(8,128)(2,1)}, u32[]{:S(2)}, u32[]{:S(2)}) collective-permute-start(bf16[1024,512]{1,0:T(8,128)(2,1)} %add_convert_fusion), channel_id=1, source_target_pairs={{0,2},{1,3},{2,0},{3,1},{4,6},{5,7},{6,4},{7,5},{8,10},{9,11},{10,... | collective-permute-start | bytes 3145736 | tf_op jit(solution)/shard_map/ppermute | solution.py:25
  67.7 19.3 %all-to-all-start.1 = ((bf16[4,128,1024]{2,1,0:T(8,128)(2,1)}), bf16[4,128,1024]{2,1,0:T(8,128)(2,1)S(1)}, u32[]{:S(2)}, u32[]{:S(2)}) async-start(bf16[4,128,1024]{2,1,0:T(8,128)(2,1)} %bitcast.22), calls=%async_computation.1 | async-start | bytes 2097152 | tf_op jit(solution)/shard_map/all_to_all | solution.py:29
  72.5 6.5 %collective-permute-start.9 = (f32[8,512]{1,0:T(8,128)S(1)}, f32[8,512]{1,0:T(8,128)S(1)}, u32[]{:S(2)}, u32[]{:S(2)}) collective-permute-start(f32[8,512]{1,0:T(8,128)S(1)} %add.30), channel_id=1, source_target_pairs={{0,64},{16,80},{32,96},{48,112},{64,0},{80,16},{96,32},{112,48},{1... | collective-permute-start | bytes 49160 | tf_op jit(solution)/shard_map/ppermute | solution.py:161
  79.0 5.6 %collective-permute-start.10 = (f32[8,512]{1,0:T(8,128)S(1)}, f32[8,512]{1,0:T(8,128)S(1)}, u32[]{:S(2)}, u32[]{:S(2)}) collective-permute-start(f32[8,512]{1,0:T(8,128)S(1)} %add.33), channel_id=1, source_target_pairs={{0,32},{16,48},{32,0},{48,16},{64,96},{80,112},{96,64},{112,80},{1... | collective-permute-start | bytes 49160 | tf_op jit(solution)/shard_map/ppermute | solution.py:161

commit v4 on v3

--- a/solution.py
+++ b/solution.py
@@ -91,10 +91,13 @@
     )(pick, total, frags, anchor, velocity)
 
 
-def finish_kernel(base, other, parts, own, keys, held, result, held_parts, held_keys, sems, out_sems):
+def finish_kernel(base, other, parts, own, keys, held_base, held, result, held_parts, held_keys, sems, out_sems):
     chunks, rows = held.shape[:2]
     blocks, amount, tall = held_parts.shape[:3]
-    copies = [(other.at[pl.ds(c * rows, rows)], held.at[c]) for c in range(chunks)]
+    copies = []
+    for c in range(chunks):
+        part = pl.ds(c * rows, rows)
+        copies += [(base.at[part], held_base.at[c]), (other.at[part], held.at[c])]
     copies += [(parts.at[:, pl.ds(n * tall, tall)], held_parts.at[n]) for n in range(blocks)]
     copies = [pltpu.make_async_copy(source, to, sems.at[n]) for n, (source, to) in enumerate(copies)]
     for copy in copies:
@@ -106,12 +109,13 @@
         outs[-1].start()
 
     for c in range(chunks):
-        copies[c].wait()
+        copies[2 * c].wait()
+        copies[2 * c + 1].wait()
         part = pl.ds(c * rows, rows)
-        result[c] = (base[part] + held[c].astype(jnp.float32)).astype(jnp.bfloat16)
+        result[c] = (held_base[c] + held[c].astype(jnp.float32)).astype(jnp.bfloat16)
         leave(result.at[c], own.at[part])
     for n in range(blocks):
-        copies[chunks + n].wait()
+        copies[2 * chunks + n].wait()
         total = held_parts[n, 0].astype(jnp.float32)
         for part in range(1, amount):
             total = total + held_parts[n, part].astype(jnp.float32)
@@ -128,14 +132,15 @@
     return pl.pallas_call(
         finish_kernel,
         out_shape=[jax.ShapeDtypeStruct((rows, cols), bf16), jax.ShapeDtypeStruct((count, features), bf16)],
-        in_specs=[pl.BlockSpec(memory_space=pltpu.VMEM)] + [pl.BlockSpec(memory_space=pl.ANY)] * 2,
+        in_specs=[pl.BlockSpec(memory_space=pl.ANY)] * 3,
         out_specs=[pl.BlockSpec(memory_space=pl.ANY)] * 2,
         scratch_shapes=[
+            pltpu.VMEM((chunks, rows // chunks, cols), jnp.float32),
             pltpu.VMEM((chunks, rows // chunks, cols), bf16),
             pltpu.VMEM((chunks, rows // chunks, cols), bf16),
             pltpu.VMEM((blocks, amount, count // blocks, features), bf16),
             pltpu.VMEM((blocks, count // blocks, features), bf16),
-            pltpu.SemaphoreType.DMA((blocks + chunks,)),
+            pltpu.SemaphoreType.DMA((blocks + 2 * chunks,)),
             pltpu.SemaphoreType.DMA((blocks + chunks,)),
         ],
         compiler_params=pltpu.CompilerParams(vmem_limit_bytes=10 << 20),

time: 90.4 us -> 90.5 us (level)
  no operation moved by 1% of the time
where the time goes in v4:
time: 90.5 us; the launch traced here: 89.8 us
  starting transfers between devices  55.8 us (62%)
  waiting for transfers between devices  11.9 us (13%)
  matrix products  11.8 us (13%)
  Pallas kernels  7.03 us (8%)
  other arithmetic  1.35 us (1%)
  local copies, waits for them, and re-layouts  1.08 us (1%)
  between operations  0.91 us (1%)
    ppermute x5, starting transfers between devices, double(): lax.ppermute(total, 'rep', [(i, i ^ bit) for i in range(replicas)])  27.3 us
    all_to_all x2, starting transfers between devices, exchange(): return lax.all_to_all(value, 'fsdp', 0, 0, axis_index_groups=SAME_SEAT)  14.4 us
    ppermute x6, starting transfers between devices, send(): return lax.ppermute(value, 'fsdp', pairs)  14.1 us
    ppermute x5, waiting for transfers between devices, double(): lax.ppermute(total, 'rep', [(i, i ^ bit) for i in range(replicas)])  11.3 us
    dot_general x4, matrix products, grad(): jnp.einsum('tk,tc->kc', cot, got[:, k * piece:(k + 1) * piece], preferred...  6.76 us
    dot_general x1, matrix products, local(): jnp.einsum('tc,kc->tk', got[:, :SEATS * piece], weights, preferred_elemen...  5.01 us
    pallas_call x1, Pallas kernels, pack(): pl.pallas_call(functools.partial(pack_kernel, scale, cuts), grid=(count /...  3.02 us
    pallas_call x1, Pallas kernels, finish(): pl.pallas_call(finish_kernel, out_shape=[jax.ShapeDtypeStruct((rows, cols...  2.22 us
  transfers between devices with their start and end apart: 13, of which 6 were waited for; matrix products, arithmetic and copies ran while one was open for 14% of the time, Pallas kernels for 2%

profile of v4, /device:TPU:8, one launch (start us, length us, event | category | flops | bytes accessed | tf_op | source)
XLA Modules:
  0.0 89.8 jit_solution(3054929222483624902)
XLA Ops:
  0.6 3.0 %pack.1 = bf16[4,128,3072]{2,1,0:T(8,128)(2,1)} custom-call(bf16[128,8192]{1,0:T(8,128)(2,1)} %bitcast.21, bf16[128,1024]{1,0:T(8,128)(2,1)} %bitcast.23), custom_call_target="tpu_custom_call" | custom-call | bytes 6291456 | tf_op jit(solution)/shard_map/pack/pallas_call | solution.py:56
  3.7 9.6 %all-to-all-start = ((bf16[4,128,3072]{2,1,0:T(8,128)(2,1)}), bf16[4,128,3072]{2,1,0:T(8,128)(2,1)S(1)}, u32[]{:S(2)}, u32[]{:S(2)}) async-start(bf16[4,128,3072]{2,1,0:T(8,128)(2,1)} %pack.1), calls=%async_computation | async-start | bytes 6291456 | tf_op jit(solution)/shard_map/all_to_all | solution.py:29
  13.3 1.9 %collective-permute-start.3 = (bf16[1024,512]{1,0:T(8,128)(2,1)}, bf16[1024,512]{1,0:T(8,128)(2,1)}, u32[]{:S(2)}, u32[]{:S(2)}) collective-permute-start(bf16[1024,512]{1,0:T(8,128)(2,1)} %bitcast.28), channel_id=1, source_target_pairs={{0,2},{1,3},{2,0},{3,1},{4,6},{5,7},{6,4},{7,5},{8,10},{9,11},{10,... | collective-permute-start | bytes 3145736 | tf_op jit(solution)/shard_map/ppermute | solution.py:25
  16.0 14.1 %collective-permute-start.1 = (f32[8,512]{1,0:T(8,128)S(1)}, f32[8,512]{1,0:T(8,128)S(1)}, u32[]{:S(2)}, u32[]{:S(2)}) collective-permute-start(f32[8,512]{1,0:T(8,128)S(1)} %convert_subtract_fusion), channel_id=1, source_target_pairs={{0,256},{16,272},{32,288},{48,304},{64,320},{80,336},{96,352},{112... | collective-permute-start | bytes 49160 | tf_op jit(solution)/shard_map/ppermute | solution.py:166
  30.2 1.7 %collective-permute-done.1 = f32[8,512]{1,0:T(8,128)S(1)} collective-permute-done((f32[8,512]{1,0:T(8,128)S(1)}, f32[8,512]{1,0:T(8,128)S(1)}, u32[]{:S(2)}, u32[]{:S(2)}) %collective-permute-start.1) | collective-permute-done | bytes 16416 | tf_op jit(solution)/shard_map/ppermute | solution.py:166
  31.9 6.0 %collective-permute-start.2 = (f32[8,512]{1,0:T(8,128)S(1)}, f32[8,512]{1,0:T(8,128)S(1)}, u32[]{:S(2)}, u32[]{:S(2)}) collective-permute-start(f32[8,512]{1,0:T(8,128)S(1)} %add.28), channel_id=1, source_target_pairs={{0,128},{16,144},{32,160},{48,176},{64,192},{80,208},{96,224},{112... | collective-permute-start | bytes 49160 | tf_op jit(solution)/shard_map/ppermute | solution.py:166
  37.9 1.9 %collective-permute-start = (bf16[1024,512]{1,0:T(8,128)(2,1)}, bf16[1024,512]{1,0:T(8,128)(2,1)S(1)}, u32[]{:S(2)}, u32[]{:S(2)}) collective-permute-start(bf16[1024,512]{1,0:T(8,128)(2,1)} %bitcast.29), channel_id=1, source_target_pairs={{0,1},{1,0},{2,3},{3,2},{4,5},{5,4},{6,7},{7,6},{8,9},{9,8},{10,11... | collective-permute-start | bytes 3145736 | tf_op jit(solution)/shard_map/ppermute | solution.py:25
  39.9 1.6 %collective-permute-done.2 = f32[8,512]{1,0:T(8,128)S(1)} collective-permute-done((f32[8,512]{1,0:T(8,128)S(1)}, f32[8,512]{1,0:T(8,128)S(1)}, u32[]{:S(2)}, u32[]{:S(2)}) %collective-permute-start.2) | collective-permute-done | bytes 16416 | tf_op jit(solution)/shard_map/ppermute | solution.py:166
  41.4 1.9 %collective-permute-start.4 = (bf16[1024,512]{1,0:T(8,128)(2,1)}, bf16[1024,512]{1,0:T(8,128)(2,1)}, u32[]{:S(2)}, u32[]{:S(2)}) collective-permute-start(bf16[1024,512]{1,0:T(8,128)(2,1)} %collective-permute-done.3), channel_id=1, source_target_pairs={{0,1},{1,0},{2,3},{3,2},{4,5},{5,4},{6,7},{7,6},{8,9},{9,8},{10,11... | collective-permute-start | bytes 3145736 | tf_op jit(solution)/shard_map/ppermute | solution.py:25
  43.4 2.5 %collective-permute-start.5 = (f32[8,512]{1,0:T(8,128)S(1)}, f32[8,512]{1,0:T(8,128)S(1)}, u32[]{:S(2)}, u32[]{:S(2)}) collective-permute-start(f32[8,512]{1,0:T(8,128)S(1)} %add.29), channel_id=1, source_target_pairs={{0,16},{16,0},{32,48},{48,32},{64,80},{80,64},{96,112},{112,96},{1... | collective-permute-start | bytes 49160 | tf_op jit(solution)/shard_map/ppermute | solution.py:166
  45.9 3.1 %collective-permute-done.5 = f32[8,512]{1,0:T(8,128)S(1)} collective-permute-done((f32[8,512]{1,0:T(8,128)S(1)}, f32[8,512]{1,0:T(8,128)S(1)}, u32[]{:S(2)}, u32[]{:S(2)}) %collective-permute-start.5) | collective-permute-done | bytes 16416 | tf_op jit(solution)/shard_map/ppermute | solution.py:166
  50.8 1.9 %collective-permute-start.7 = (bf16[1024,512]{1,0:T(8,128)(2,1)S(1)}, bf16[1024,512]{1,0:T(8,128)(2,1)S(1)}, u32[]{:S(2)}, u32[]{:S(2)}) collective-permute-start(bf16[1024,512]{1,0:T(8,128)(2,1)S(1)} %convolution_convert_fusion), channel_id=1, source_target_pairs={{0,1},{1,0},{2,3},{3,2},{4,5},{5,4},{6,7},{7,6},{8,9},{9,8},{10,11... | collective-permute-start | bytes 3145736 | tf_op jit(solution)/shard_map/ppermute | solution.py:25
  52.8 1.7 %convolution_convert_fusion.1 = bf16[1024,512]{1,0:T(8,128)(2,1)} fusion(bf16[512,3072]{1,0:T(8,128)(2,1)S(1)} %bitcast.17), kind=kOutput, calls=%fused_computation.13 | convolution fusion | flops 537395200 | bytes 2621440 | tf_op jit(solution)/shard_map/tk,tc->kc/dot_general | solution.py:182
  54.5 2.5 %collective-permute-start.6 = (bf16[1024,512]{1,0:T(8,128)(2,1)}, bf16[1024,512]{1,0:T(8,128)(2,1)}, u32[]{:S(2)}, u32[]{:S(2)}) collective-permute-start(bf16[1024,512]{1,0:T(8,128)(2,1)} %convolution_convert_fusion.1), channel_id=1, source_target_pairs={{0,1},{1,0},{2,3},{3,2},{4,5},{5,4},{6,7},{7,6},{8,9},{9,8},{10,11... | collective-permute-start | bytes 3145736 | tf_op jit(solution)/shard_map/ppermute | solution.py:25
  57.0 1.7 %add_convert_fusion = bf16[1024,512]{1,0:T(8,128)(2,1)} fusion(bf16[1024,512]{1,0:T(8,128)(2,1)S(1)} %collective-permute-done.7, bf16[512,3072]{1,0:T(8,128)(2,1)S(1)} %bitcast.18), kind=kOutput, calls=%fused_computation.9 | convolution fusion | flops 538443776 | bytes 3670016 | tf_op jit(solution)/shard_map/tk,tc->kc/dot_general | solution.py:182
  58.8 3.9 %collective-permute-start.8 = (bf16[1024,512]{1,0:T(8,128)(2,1)}, bf16[1024,512]{1,0:T(8,128)(2,1)}, u32[]{:S(2)}, u32[]{:S(2)}) collective-permute-start(bf16[1024,512]{1,0:T(8,128)(2,1)} %add_convert_fusion), channel_id=1, source_target_pairs={{0,2},{1,3},{2,0},{3,1},{4,6},{5,7},{6,4},{7,5},{8,10},{9,11},{10,... | collective-permute-start | bytes 3145736 | tf_op jit(solution)/shard_map/ppermute | solution.py:25
  62.7 5.0 %fusion.9 = bf16[512,1024]{1,0:T(8,128)(2,1)} fusion(bf16[1024,512]{1,0:T(8,128)(2,1)} %collective-permute-done.4, bf16[1024,512]{1,0:T(8,128)(2,1)} %collective-permute-done.3, bf16[1024,512]{1,0:T(8,128)(2,1)S(1)} %copy-done.4, bf16[1024,512]{1,0:T(8,128)(2,1)S(1)} %bitcast.30, bf16[512,3072]{1,0:T(8,128)(2,1)S(1)} %bitcast.19), kind=kOutput, calls=%fused_computation.11 | convolution fusion | flops 2164785152 | bytes 7340032 | tf_op jit(solution)/shard_map/tc,kc->tk/dot_general | solution.py:190
  67.7 4.8 %all-to-all-start.1 = ((bf16[4,128,1024]{2,1,0:T(8,128)(2,1)}), bf16[4,128,1024]{2,1,0:T(8,128)(2,1)S(1)}, u32[]{:S(2)}, u32[]{:S(2)}) async-start(bf16[4,128,1024]{2,1,0:T(8,128)(2,1)} %bitcast.22), calls=%async_computation.1 | async-start | bytes 2097152 | tf_op jit(solution)/shard_map/all_to_all | solution.py:29
  72.5 2.7 %collective-permute-start.9 = (f32[8,512]{1,0:T(8,128)S(1)}, f32[8,512]{1,0:T(8,128)S(1)}, u32[]{:S(2)}, u32[]{:S(2)}) collective-permute-start(f32[8,512]{1,0:T(8,128)S(1)} %add.30), channel_id=1, source_target_pairs={{0,64},{16,80},{32,96},{48,112},{64,0},{80,16},{96,32},{112,48},{1... | collective-permute-start | bytes 49160 | tf_op jit(solution)/shard_map/ppermute | solution.py:166
  75.2 3.8 %collective-permute-done.9 = f32[8,512]{1,0:T(8,128)S(1)} collective-permute-done((f32[8,512]{1,0:T(8,128)S(1)}, f32[8,512]{1,0:T(8,128)S(1)}, u32[]{:S(2)}, u32[]{:S(2)}) %collective-permute-start.9) | collective-permute-done | bytes 16416 | tf_op jit(solution)/shard_map/ppermute | solution.py:166
  79.0 1.9 %collective-permute-start.10 = (f32[8,512]{1,0:T(8,128)S(1)}, f32[8,512]{1,0:T(8,128)S(1)}, u32[]{:S(2)}, u32[]{:S(2)}) collective-permute-start(f32[8,512]{1,0:T(8,128)S(1)} %add.33), channel_id=1, source_target_pairs={{0,32},{16,48},{32,0},{48,16},{64,96},{80,112},{96,64},{112,80},{1... | collective-permute-start | bytes 49160 | tf_op jit(solution)/shard_map/ppermute | solution.py:166
  80.9 2.6 %convert_add_fusion.base = f32[1024,512]{1,0:T(8,128)S(1)} fusion(bf16[1024,512]{1,0:T(8,128)(2,1)} %collective-permute-done.6, bf16[512,3072]{1,0:T(8,128)(2,1)} %bitcast.20), kind=kOutput, calls=%fused_computation.10 | convolution fusion | flops 537919488 | bytes 4718592 | tf_op jit(solution)/shard_map/tk,tc->kc/dot_general | solution.py:182
  85.3 1.8 %update.1 = (bf16[8,8,512]{2,1,0:T(8,128)(2,1)}, f32[8,8,512]{2,1,0:T(8,128)}, f32[8,8,512]{2,1,0:T(8,128)}) custom-call(s32[8]{0:T(128)} %pick.1, f32[8,512]{1,0:T(8,128)} %add.34.total, bf16[8,8,512]{2,1,0:T(8,128)(2,1)} %bitcast.24, f32[8,8,512]{2,1,0:T(8,128)} %anchor.1, f32[8,8,512]{2,1,0:T(8,128)} %velocity.1), custom_call_target="tpu_custom_call" | custom-call | tf_op jit(solution)/shard_map/update/pallas_call | solution.py:85
  87.5 2.2 %finish.1 = (bf16[1024,512]{1,0:T(8,128)(2,1)}, bf16[128,1024]{1,0:T(8,128)(2,1)}) custom-call(f32[1024,512]{1,0:T(8,128)S(1)} %convert_add_fusion.base, bf16[1024,512]{1,0:T(8,128)(2,1)} %collective-permute-done.8.other, bf16[4,128,1024]{2,1,0:T(8,128)(2,1)S(1)} %all-to-all-done.1.parts), custom_call_target="tpu_custom_call" | custom-call | flops 1048576 | bytes 6291456 | tf_op jit(solution)/shard_map/finish/pallas_call | solution.py:132
  (26 shorter events, 4.8 us)
Async XLA Ops:
  3.7 11.5 %copy-start.1 = (s32[8]{0:T(128)S(1)}, s32[8]{0:T(128)}, u32[]{:S(2)}) copy-start(s32[8]{0:T(128)} %pick.1) | copy-start | bytes 100
  3.7 46.4 %all-to-all-start = ((bf16[4,128,3072]{2,1,0:T(8,128)(2,1)}), bf16[4,128,3072]{2,1,0:T(8,128)(2,1)S(1)}, u32[]{:S(2)}, u32[]{:S(2)}) async-start(bf16[4,128,3072]{2,1,0:T(8,128)(2,1)} %pack.1), calls=%async_computation | async-start | bytes 6291456 | tf_op jit(solution)/shard_map/all_to_all | solution.py:29
  13.3 28.2 %collective-permute-start.3 = (bf16[1024,512]{1,0:T(8,128)(2,1)}, bf16[1024,512]{1,0:T(8,128)(2,1)}, u32[]{:S(2)}, u32[]{:S(2)}) collective-permute-start(bf16[1024,512]{1,0:T(8,128)(2,1)} %bitcast.28), channel_id=1, source_target_pairs={{0,2},{1,3},{2,0},{3,1},{4,6},{5,7},{6,4},{7,5},{8,10},{9,11},{10,... | collective-permute-start | bytes 3145736 | tf_op jit(solution)/shard_map/ppermute | solution.py:25
  16.0 15.9 %collective-permute-start.1 = (f32[8,512]{1,0:T(8,128)S(1)}, f32[8,512]{1,0:T(8,128)S(1)}, u32[]{:S(2)}, u32[]{:S(2)}) collective-permute-start(f32[8,512]{1,0:T(8,128)S(1)} %convert_subtract_fusion), channel_id=1, source_target_pairs={{0,256},{16,272},{32,288},{48,304},{64,320},{80,336},{96,352},{112... | collective-permute-start | bytes 49160 | tf_op jit(solution)/shard_map/ppermute | solution.py:166
  31.9 9.5 %collective-permute-start.2 = (f32[8,512]{1,0:T(8,128)S(1)}, f32[8,512]{1,0:T(8,128)S(1)}, u32[]{:S(2)}, u32[]{:S(2)}) collective-permute-start(f32[8,512]{1,0:T(8,128)S(1)} %add.28), channel_id=1, source_target_pairs={{0,128},{16,144},{32,160},{48,176},{64,192},{80,208},{96,224},{112... | collective-permute-start | bytes 49160 | tf_op jit(solution)/shard_map/ppermute | solution.py:166
  37.9 11.1 %collective-permute-start = (bf16[1024,512]{1,0:T(8,128)(2,1)}, bf16[1024,512]{1,0:T(8,128)(2,1)S(1)}, u32[]{:S(2)}, u32[]{:S(2)}) collective-permute-start(bf16[1024,512]{1,0:T(8,128)(2,1)} %bitcast.29), channel_id=1, source_target_pairs={{0,1},{1,0},{2,3},{3,2},{4,5},{5,4},{6,7},{7,6},{8,9},{9,8},{10,11... | collective-permute-start | bytes 3145736 | tf_op jit(solution)/shard_map/ppermute | solution.py:25
  41.4 8.6 %collective-permute-start.4 = (bf16[1024,512]{1,0:T(8,128)(2,1)}, bf16[1024,512]{1,0:T(8,128)(2,1)}, u32[]{:S(2)}, u32[]{:S(2)}) collective-permute-start(bf16[1024,512]{1,0:T(8,128)(2,1)} %collective-permute-done.3), channel_id=1, source_target_pairs={{0,1},{1,0},{2,3},{3,2},{4,5},{5,4},{6,7},{7,6},{8,9},{9,8},{10,11... | collective-permute-start | bytes 3145736 | tf_op jit(solution)/shard_map/ppermute | solution.py:25
  43.4 5.6 %collective-permute-start.5 = (f32[8,512]{1,0:T(8,128)S(1)}, f32[8,512]{1,0:T(8,128)S(1)}, u32[]{:S(2)}, u32[]{:S(2)}) collective-permute-start(f32[8,512]{1,0:T(8,128)S(1)} %add.29), channel_id=1, source_target_pairs={{0,16},{16,0},{32,48},{48,32},{64,80},{80,64},{96,112},{112,96},{1... | collective-permute-start | bytes 49160 | tf_op jit(solution)/shard_map/ppermute | solution.py:166
  49.0 1.1 %copy-start.3 = (bf16[1024,512]{1,0:T(8,128)(2,1)}, bf16[1024,512]{1,0:T(8,128)(2,1)S(1)}, u32[]{:S(2)}) copy-start(bf16[1024,512]{1,0:T(8,128)(2,1)S(1)} %collective-permute-done) | copy-start | bytes 3145732
  50.1 12.6 %copy-start = (bf16[4,128,3072]{2,1,0:T(8,128)(2,1)}, bf16[4,128,3072]{2,1,0:T(8,128)(2,1)S(1)}, u32[]{:S(2)}) copy-start(bf16[4,128,3072]{2,1,0:T(8,128)(2,1)S(1)} %all-to-all-done) | copy-start | bytes 9437188
  50.8 6.2 %collective-permute-start.7 = (bf16[1024,512]{1,0:T(8,128)(2,1)S(1)}, bf16[1024,512]{1,0:T(8,128)(2,1)S(1)}, u32[]{:S(2)}, u32[]{:S(2)}) collective-permute-start(bf16[1024,512]{1,0:T(8,128)(2,1)S(1)} %convolution_convert_fusion), channel_id=1, source_target_pairs={{0,1},{1,0},{2,3},{3,2},{4,5},{5,4},{6,7},{7,6},{8,9},{9,8},{10,11... | collective-permute-start | bytes 3145736 | tf_op jit(solution)/shard_map/ppermute | solution.py:25
  54.5 8.2 %copy-start.2 = (bf16[1,1024,512]{2,1,0:T(8,128)(2,1)S(1)}, bf16[1,1024,512]{2,1,0:T(8,128)(2,1)}, u32[]{:S(2)}) copy-start(bf16[1,1024,512]{2,1,0:T(8,128)(2,1)} %param.8) | copy-start | bytes 3145732
  54.5 8.2 %copy-start.4 = (bf16[1024,512]{1,0:T(8,128)(2,1)S(1)}, bf16[1024,512]{1,0:T(8,128)(2,1)}, u32[]{:S(2)}) copy-start(bf16[1024,512]{1,0:T(8,128)(2,1)} %copy-done.3) | copy-start | bytes 3145732
  54.5 18.0 %collective-permute-start.6 = (bf16[1024,512]{1,0:T(8,128)(2,1)}, bf16[1024,512]{1,0:T(8,128)(2,1)}, u32[]{:S(2)}, u32[]{:S(2)}) collective-permute-start(bf16[1024,512]{1,0:T(8,128)(2,1)} %convolution_convert_fusion.1), channel_id=1, source_target_pairs={{0,1},{1,0},{2,3},{3,2},{4,5},{5,4},{6,7},{7,6},{8,9},{9,8},{10,11... | collective-permute-start | bytes 3145736 | tf_op jit(solution)/shard_map/ppermute | solution.py:25
  58.8 28.8 %collective-permute-start.8 = (bf16[1024,512]{1,0:T(8,128)(2,1)}, bf16[1024,512]{1,0:T(8,128)(2,1)}, u32[]{:S(2)}, u32[]{:S(2)}) collective-permute-start(bf16[1024,512]{1,0:T(8,128)(2,1)} %add_convert_fusion), channel_id=1, source_target_pairs={{0,2},{1,3},{2,0},{3,1},{4,6},{5,7},{6,4},{7,5},{8,10},{9,11},{10,... | collective-permute-start | bytes 3145736 | tf_op jit(solution)/shard_map/ppermute | solution.py:25
  67.7 19.3 %all-to-all-start.1 = ((bf16[4,128,1024]{2,1,0:T(8,128)(2,1)}), bf16[4,128,1024]{2,1,0:T(8,128)(2,1)S(1)}, u32[]{:S(2)}, u32[]{:S(2)}) async-start(bf16[4,128,1024]{2,1,0:T(8,128)(2,1)} %bitcast.22), calls=%async_computation.1 | async-start | bytes 2097152 | tf_op jit(solution)/shard_map/all_to_all | solution.py:29
  72.5 6.5 %collective-permute-start.9 = (f32[8,512]{1,0:T(8,128)S(1)}, f32[8,512]{1,0:T(8,128)S(1)}, u32[]{:S(2)}, u32[]{:S(2)}) collective-permute-start(f32[8,512]{1,0:T(8,128)S(1)} %add.30), channel_id=1, source_target_pairs={{0,64},{16,80},{32,96},{48,112},{64,0},{80,16},{96,32},{112,48},{1... | collective-permute-start | bytes 49160 | tf_op jit(solution)/shard_map/ppermute | solution.py:166
  79.0 5.6 %collective-permute-start.10 = (f32[8,512]{1,0:T(8,128)S(1)}, f32[8,512]{1,0:T(8,128)S(1)}, u32[]{:S(2)}, u32[]{:S(2)}) collective-permute-start(f32[8,512]{1,0:T(8,128)S(1)} %add.33), channel_id=1, source_target_pairs={{0,32},{16,48},{32,0},{48,16},{64,96},{80,112},{96,64},{112,80},{1... | collective-permute-start | bytes 49160 | tf_op jit(solution)/shard_map/ppermute | solution.py:166
